TPU v7x, 32 devices: a whole 2x2x4 slice. The times are simulated.
32 devices in a mesh: rows: 8 (over z, x), cols: 4 (over y, core).
Axes of the slice: x: 2, y: 2, z: 4, core: 2. Of those that a mesh axis runs over, the one named last changes fastest.
Arguments:
- conc: float32 [8, 48, 64, 512], P(None, None, 'rows', 'cols'), may hold values from 0 to 2
- nwp: bfloat16 [2, 137, 16384], P(None, None, 'rows'), may hold values from -0.3 to 0.3
- lev_lo: int32 [48], replicated, may hold values from 0 to 135
- frac: float32 [48], replicated, may hold values from 0 to 1
- pick: int32 [8, 4, 8, 64], P('rows', 'cols'), may hold values from 0 to 2047
- corner_slot: int32 [4, 64, 512], P(None, 'rows', 'cols'), may hold values from 0 to 511
- corner_wt: float32 [4, 64, 512], P(None, 'rows', 'cols'), may hold values from 0.25 to 1
- settle: float32 [8], replicated, may hold values from 0.015 to 0.15
- source_mask: int32 [64, 512], P('rows', 'cols'), may hold values 0 or 1
- profile: float32 [8, 48], replicated, may hold values from 0.1 to 1
Outputs:
- final_conc: float32 [8, 48, 64, 512], P(None, None, 'rows', 'cols')
- deposit: float32 [8, 64, 512], P(None, 'rows', 'cols')
All inputs are finite; a program needn't handle non-finite values. No bound on the sum of `source_mask` on one device may be relied on, other than what follows from the above.
Results may differ from a plain program's by a relative error of at most 0.0013.
Values may be sent and summed in bfloat16 or wider, within the bound.
A program may use at most 128 MiB of HBM per device.

v0:
```python
import jax
import jax.numpy as jnp
from jax import lax
from jax.sharding import PartitionSpec as P

STEPS = 3


KAPPA = 0.05


def with_halo(array, sides, width):
    for axis, dim in sides:
        peers, length = (lax.axis_size(axis), array.shape[dim])
        up = [(i, (i + 1) % peers) for i in range(peers - 1)]
        down = [(j, i) for i, j in up]
        last = lax.slice_in_dim(array, length - width, length, axis=dim)
        leading = lax.slice_in_dim(array, 0, width, axis=dim)
        before = lax.ppermute(last, axis, up)
        after = lax.ppermute(leading, axis, down)
        array = jnp.concatenate([before, array, after], axis=dim)
    return array


def select_columns(columns, order):
    count = columns.shape[2]
    selector = (jnp.arange(count, dtype=jnp.int32)[:, None] == order[None, :]).astype(jnp.bfloat16)
    picked = jnp.einsum("fln,nj->flj", columns, selector, preferred_element_type=jnp.float32)
    return picked.astype(jnp.bfloat16)


def vertical(columns, lev_lo, frac):
    level_ids = jnp.arange(columns.shape[1], dtype=jnp.int32)
    lower_hit = (level_ids[None, :] == lev_lo[:, None]).astype(jnp.float32)
    upper_hit = (level_ids[None, :] == lev_lo[:, None] + 1).astype(jnp.float32)
    share = frac[:, None]
    interp = (1.0 - share) * lower_hit + share * upper_hit
    mixed = jnp.einsum(
        "kl,fln->fkn", interp, columns.astype(jnp.float32), precision=lax.Precision.HIGHEST
    )
    return mixed.astype(jnp.bfloat16)


def horizontal(levels, slots, corner_wt):
    weight_sum = jnp.sum(corner_wt, axis=0)
    norm_wt = corner_wt / weight_sum
    slot_ids = jnp.arange(levels.shape[2], dtype=jnp.int32)[:, None, None]
    table = None
    for corner in range(4):
        term = jnp.where(slot_ids == slots[corner][None], norm_wt[corner][None], 0.0)
        table = term if table is None else table + term
    return jnp.einsum(
        "fks,syx->fkyx", levels.astype(jnp.float32), table, precision=lax.Precision.HIGHEST
    )


def advance(padded, winds, emission, settle):
    east = 0.5 * (winds[0][:, :, 1:] + winds[0][:, :, :-1])
    north = 0.5 * (winds[1][:, 1:, :] + winds[1][:, :-1, :])
    flux_x = (
        jnp.maximum(east, 0.0) * padded[..., :, :-1] + jnp.minimum(east, 0.0) * padded[..., :, 1:]
    )
    flux_y = (
        jnp.maximum(north, 0.0) * padded[..., :-1, :] + jnp.minimum(north, 0.0) * padded[..., 1:, :]
    )
    div_x = (flux_x[..., 1:] - flux_x[..., :-1])[..., 1:-1, :]
    div_y = (flux_y[..., 1:, :] - flux_y[..., :-1, :])[..., :, 1:-1]
    centre = padded[..., 1:-1, 1:-1]
    lap = (
        padded[..., 2:, 1:-1]
        + padded[..., :-2, 1:-1]
        + padded[..., 1:-1, 2:]
        + padded[..., 1:-1, :-2]
        - 4.0 * centre
    )
    falling = settle[:, None, None, None] * centre
    arriving = jnp.concatenate([jnp.zeros_like(falling[:, :1]), falling[:, :-1]], axis=1)
    fresh = centre - div_x - div_y + KAPPA * lap - falling + arriving + emission
    return (fresh, falling[:, -1])


def per_device(conc, nwp, lev_lo, frac, pick, corner_slot, corner_wt, settle, source_mask, profile):
    order = pick.reshape(-1)
    received = lax.all_to_all(
        select_columns(nwp, order), "rows", split_axis=2, concat_axis=2, tiled=True
    )
    levels = vertical(received, lev_lo, frac)
    winds = horizontal(levels, corner_slot, corner_wt)
    level_count = winds.shape[1]
    row_count = conc.shape[2]
    col_count = conc.shape[3]
    flags = source_mask.astype(jnp.float32)
    stacked = jnp.concatenate(
        [winds.reshape(2 * level_count, row_count, col_count), flags[None]], axis=0
    )
    margin = STEPS
    rimmed = with_halo(stacked.astype(jnp.bfloat16), (("rows", 1), ("cols", 2)), margin).astype(
        stacked.dtype
    )
    wind_all = rimmed[: 2 * level_count].reshape(
        2, level_count, row_count + 2 * margin, col_count + 2 * margin
    )
    flag_all = rimmed[2 * level_count]
    deposit = jnp.zeros((conc.shape[0], row_count, col_count), jnp.float32)
    total_rows = row_count * lax.axis_size("rows")
    total_cols = col_count * lax.axis_size("cols")
    first_row = lax.axis_index("rows") * row_count
    first_col = lax.axis_index("cols") * col_count
    state = with_halo(conc, (("rows", 2), ("cols", 3)), margin)
    for step in range(STEPS):
        height = row_count + 2 * (margin - step)
        width = col_count + 2 * (margin - step)
        wind_now = wind_all[:, :, step : step + height, step : step + width]
        flag_now = flag_all[step + 1 : step + height - 1, step + 1 : step + width - 1]
        emission = flag_now[None, None] * profile[:, :, None, None]
        state, fallen = advance(state, wind_now, emission, settle)
        keep = margin - step - 1
        row_index = first_row - keep + jnp.arange(row_count + 2 * keep, dtype=jnp.int32)
        col_index = first_col - keep + jnp.arange(col_count + 2 * keep, dtype=jnp.int32)
        row_ok = (row_index >= 0) & (row_index < total_rows)
        col_ok = (col_index >= 0) & (col_index < total_cols)
        inside = row_ok[:, None] & col_ok[None, :]
        state = jnp.where(inside[None, None], state, 0.0)
        deposit = deposit + fallen[:, keep : keep + row_count, keep : keep + col_count]
    return (state, deposit)


def solution(mesh):
    placed = (
        P(None, None, "rows", "cols"),
        P(None, None, "rows"),
        P(),
        P(),
        P("rows", "cols", None, None),
        P(None, "rows", "cols"),
        P(None, "rows", "cols"),
        P(),
        P("rows", "cols"),
        P(),
    )
    return jax.shard_map(
        per_device,
        mesh=mesh,
        in_specs=placed,
        out_specs=(P(None, None, "rows", "cols"), P(None, "rows", "cols")),
        check_vma=False,
    )
```

profile of v0, /device:TPU:14, one launch (start us, length us, event | category | flops | bytes accessed | tf_op | source)
XLA Modules:
  0.0 262.4 jit_solution(15673923849820111996)
XLA Ops:
  4.1 6.2 %all-to-all-start = ((bf16[2,137,512]{1,0,2:T(2,128)(2,1)}), bf16[2,137,512]{1,0,2:T(2,128)(2,1)S(1)}, u32[]{:S(2)}, u32[]{:S(2)}) async-start(bf16[2,137,512]{1,0,2:T(2,128)(2,1)} %copy.85), calls=%async_computation | async-start | bytes 1048576 | tf_op jit(solution)/shard_map/all_to_all | solution.py:84
  14.0 4.3 %collective-permute-start = (f32[8,48,3,128]{3,1,2,0:T(8,128)}, f32[8,48,3,128]{3,1,2,0:T(8,128)}, u32[]{:S(2)}, u32[]{:S(2)}) collective-permute-start(f32[8,48,3,128]{3,1,2,0:T(8,128)} %copy.93), channel_id=1, source_target_pairs={{0,4},{4,8},{8,12},{12,16},{16,20},{20,24},{24,28},{1,5},{5,9},{9,... | collective-permute-start | bytes 1769480 | tf_op jit(solution)/shard_map/ppermute | solution.py:19
  24.3 4.7 %collective-permute-start.4 = (bf16[97,3,128]{2,1,0:T(4,128)(2,1)S(1)}, bf16[97,3,128]{2,1,0:T(4,128)(2,1)S(1)}, u32[]{:S(2)}, u32[]{:S(2)}) collective-permute-start(bf16[97,3,128]{2,1,0:T(4,128)(2,1)S(1)} %get-tuple-element.46), channel_id=1, source_target_pairs={{0,4},{4,8},{8,12},{12,16},{16,20},{20,24},{24,28},{1,5},{5,9},{9,... | collective-permute-start | bytes 223496 | tf_op jit(solution)/shard_map/ppermute | solution.py:19
  31.3 17.1 %collective-permute-done.4 = bf16[97,3,128]{2,1,0:T(4,128)(2,1)S(1)} collective-permute-done((bf16[97,3,128]{2,1,0:T(4,128)(2,1)S(1)}, bf16[97,3,128]{2,1,0:T(4,128)(2,1)S(1)}, u32[]{:S(2)}, u32[]{:S(2)}) %collective-permute-start.4) | collective-permute-done | bytes 74528 | tf_op jit(solution)/shard_map/ppermute | solution.py:19
  51.6 3.8 %collective-permute-start.7 = (bf16[97,14,3]{2,1,0:T(8,128)(2,1)}, bf16[97,14,3]{2,1,0:T(8,128)(2,1)S(1)}, u32[]{:S(2)}, u32[]{:S(2)}) collective-permute-start(bf16[97,14,3]{2,1,0:T(8,128)(2,1)} %get-tuple-element.45), channel_id=1, source_target_pairs={{1,0},{2,1},{3,2},{5,4},{6,5},{7,6},{9,8},{10,9},{11,10},{13,12},{... | collective-permute-start | bytes 24452 | tf_op jit(solution)/shard_map/ppermute | solution.py:20
  91.4 4.0 %collective-permute-done.2 = f32[8,48,14,3]{1,0,3,2:T(8,128)S(1)} collective-permute-done((f32[8,48,14,3]{1,0,3,2:T(8,128)}, f32[8,48,14,3]{1,0,3,2:T(8,128)S(1)}, u32[]{:S(2)}, u32[]{:S(2)}) %collective-permute-start.2) | collective-permute-done | bytes 64544 | tf_op jit(solution)/shard_map/ppermute | solution.py:19
  95.4 3.8 %copy.82 = f32[8,48,14,3]{3,2,0,1:T(8,128)} copy(f32[8,48,14,3]{1,0,3,2:T(8,128)S(1)} %collective-permute-done.2) | data formatting | bytes 129024 | tf_op jit(solution)/shard_map/ppermute | solution.py:19
  99.2 3.8 %copy.83 = f32[8,48,14,3]{3,2,0,1:T(8,128)} copy(f32[8,48,14,3]{1,0,3,2:T(8,128)S(1)} %collective-permute-done.3) | data formatting | bytes 129024 | tf_op jit(solution)/shard_map/ppermute | solution.py:20
  103.0 7.8 %pad_maximum_fusion = f32[8,48,14,134]{3,2,0,1:T(8,128)S(1)} fusion(f32[8,48,14,3]{3,2,0,1:T(8,128)} %copy.83, f32[8,48,3,128]{3,2,0,1:T(4,128)} %copy-done.3, f32[8,48,3,128]{3,2,0,1:T(4,128)} %copy-done.4, f32[8,48,14,3]{3,2,0,1:T(8,128)} %copy.82, f32[8,48,8,128]{3,2,1,0:T(8,128)} %param.10), kind=kLoop, calls=%fused_computation.46 | loop fusion | flops 2881536 | bytes 5763072 | tf_op jit(solution)/shard_map/concatenate | solution.py:21
  116.1 5.0 %fusion.21 = f32[8,48,13,134]{3,2,0,1:T(8,128)} fusion(f32[8,48,14,134]{3,2,0,1:T(8,128)S(1)} %pad_maximum_fusion, f32[48,13,134]{2,1,0:T(8,128)S(1)} %copy-done.10, f32[48,13,134]{2,1,0:T(8,128)S(1)} %copy-done.9), kind=kLoop, calls=%fused_computation.39 | loop fusion | flops 2006784 | bytes 8696064 | tf_op jit(solution)/shard_map/add | solution.py:64
  121.1 11.8 %fusion.94 = (f32[8,48,12,134]{3,2,0,1:T(8,128)}, f32[8,48,12,134]{3,2,0,1:T(8,128)}) fusion(f32[8,48,13,134]{3,2,0,1:T(8,128)} %fusion.21), kind=kLoop, calls=%fused_computation.178 | loop fusion | bytes 9879552 | tf_op jit(solution)/shard_map/slice | solution.py:67
  132.9 6.6 %fusion.23 = f32[8,48,14,133]{3,2,0,1:T(8,128)} fusion(f32[8,48,14,134]{3,2,0,1:T(8,128)S(1)} %pad_maximum_fusion, f32[48,14,133]{2,1,0:T(8,128)} %get-tuple-element.27, f32[48,14,133]{2,1,0:T(8,128)} %get-tuple-element.26), kind=kLoop, calls=%fused_computation.44 | loop fusion | flops 2145024 | bytes 9295104 | tf_op jit(solution)/shard_map/add | solution.py:61
  139.5 11.1 %fusion.93 = (f32[8,48,14,132]{3,2,0,1:T(8,128)}, f32[8,48,14,132]{3,2,0,1:T(8,128)}) fusion(f32[8,48,14,133]{3,2,0,1:T(8,128)} %fusion.23), kind=kLoop, calls=%fused_computation.177 | loop fusion | bytes 11354112 | tf_op jit(solution)/shard_map/slice | solution.py:66
  150.6 18.0 %fusion.19 = f32[8,48,12,132]{3,2,0,1:T(8,128)} fusion(f32[8,48,14,134]{3,2,0,1:T(8,128)S(1)} %pad_maximum_fusion, f32[8,48,12,134]{3,2,0,1:T(8,128)} %get-tuple-element.23, f32[8,48,12,134]{3,2,0,1:T(8,128)} %get-tuple-element.22, f32[8,48,14,132]{3,2,0,1:T(8,128)} %get-tuple-element.21, f32[8,48,14,132]{3,2,0,1:T(8,128)} %get-tuple-element.20, ...), kind=kLoop, calls=%fused_computation.33 | loop fusion | flops 10340352 | bytes 26722064 | tf_op jit(solution)/shard_map/jit(_where)/select_n | solution.py:123
  168.6 4.5 %slice_multiply_fusion.12 = f32[8,48,10,130]{3,2,0,1:T(8,128)S(1)} fusion(f32[8,48,12,132]{3,2,0,1:T(8,128)} %fusion.19, f32[8]{0:T(128)S(1)} %copy-done.15), kind=kLoop, calls=%fused_computation.47 | loop fusion | flops 499200 | bytes 3993632 | tf_op jit(solution)/shard_map/mul | solution.py:76
  173.2 3.9 %slice.439 = f32[8,47,10,130]{3,2,0,1:T(8,128)} slice(f32[8,48,10,130]{3,2,0,1:T(8,128)S(1)} %slice_multiply_fusion.12), slice={[0:8], [0:47], [0:10], [0:130]} | slice | bytes 3910400 | tf_op jit(solution)/shard_map/slice | solution.py:77
  178.7 5.0 %fusion.10 = f32[8,48,11,132]{3,2,0,1:T(8,128)} fusion(f32[8,48,12,132]{3,2,0,1:T(8,128)S(1)} %bitcast.65, f32[48,11,132]{2,1,0:T(8,128)S(1)} %copy-done.8, f32[48,11,132]{2,1,0:T(8,128)S(1)} %copy-done.7), kind=kLoop, calls=%fused_computation.19 | loop fusion | flops 1672704 | bytes 7248384 | tf_op jit(solution)/shard_map/add | solution.py:64
  183.7 11.8 %fusion.92 = (f32[8,48,10,132]{3,2,0,1:T(8,128)}, f32[8,48,10,132]{3,2,0,1:T(8,128)}) fusion(f32[8,48,11,132]{3,2,0,1:T(8,128)} %fusion.10), kind=kLoop, calls=%fused_computation.176 | loop fusion | bytes 8110080 | tf_op jit(solution)/shard_map/slice | solution.py:67
  195.5 6.6 %fusion.12 = f32[8,48,12,131]{3,2,0,1:T(8,128)} fusion(f32[8,48,12,132]{3,2,0,1:T(8,128)S(1)} %bitcast.65, f32[48,12,131]{2,1,0:T(8,128)} %get-tuple-element.41, f32[48,12,131]{2,1,0:T(8,128)} %get-tuple-element.40), kind=kLoop, calls=%fused_computation.24 | loop fusion | flops 1810944 | bytes 7847424 | tf_op jit(solution)/shard_map/add | solution.py:61
  202.0 11.0 %fusion.91 = (f32[8,48,12,130]{3,2,0,1:T(8,128)}, f32[8,48,12,130]{3,2,0,1:T(8,128)}) fusion(f32[8,48,12,131]{3,2,0,1:T(8,128)} %fusion.12), kind=kLoop, calls=%fused_computation.175 | loop fusion | bytes 9584640 | tf_op jit(solution)/shard_map/slice | solution.py:66
  213.1 18.1 %fusion.8 = f32[8,48,10,130]{3,2,0,1:T(8,128)} fusion(f32[8,48,12,132]{3,2,0,1:T(8,128)S(1)} %bitcast.65, f32[8,48,10,132]{3,2,0,1:T(8,128)} %get-tuple-element.19, f32[8,48,10,132]{3,2,0,1:T(8,128)} %get-tuple-element.18, f32[8,48,12,130]{3,2,0,1:T(8,128)} %get-tuple-element.17, f32[8,48,12,130]{3,2,0,1:T(8,128)} %get-tuple-element.16, ...), kind=kLoop, calls=%fused_computation.13 | loop fusion | flops 8486400 | bytes 21931268 | tf_op jit(solution)/shard_map/jit(_where)/select_n | solution.py:123
  234.5 8.1 %fusion.1 = f32[8,48,10,129]{3,2,0,1:T(8,128)S(1)} fusion(f32[8,48,10,130]{3,2,0,1:T(8,128)} %fusion.8, f32[48,10,129]{2,1,0:T(8,128)} %get-tuple-element.37, f32[48,10,129]{2,1,0:T(8,128)} %get-tuple-element.36), kind=kLoop, calls=%fused_computation.4 | loop fusion | flops 1486080 | bytes 6439680 | tf_op jit(solution)/shard_map/add | solution.py:61
  242.6 3.9 %fusion.89 = (f32[8,48,10,128]{3,2,0,1:T(8,128)}, f32[8,48,10,128]{3,2,0,1:T(8,128)}) fusion(f32[8,48,10,129]{3,2,0,1:T(8,128)S(1)} %fusion.1), kind=kLoop, calls=%fused_computation.173 | loop fusion | bytes 7864320 | tf_op jit(solution)/shard_map/slice | solution.py:66
  253.9 6.4 %fusion.43 = f32[8,48,8,128]{3,2,0,1:T(8,128)S(1)} fusion(f32[8,48,10,130]{3,2,0,1:T(8,128)S(1)} %bitcast.67, f32[8,48,8,130]{3,2,0,1:T(8,128)} %get-tuple-element.15, f32[8,48,8,130]{3,2,0,1:T(8,128)} %get-tuple-element.14, f32[8,48,10,128]{3,2,0,1:T(8,128)} %get-tuple-element.13, f32[8,48,10,128]{3,2,0,1:T(8,128)} %get-tuple-element.12, ...), kind=kLoop, calls=%fused_computation.74 | loop fusion | flops 6684672 | bytes 17275424 | tf_op jit(solution)/shard_map/jit(_where)/select_n | solution.py:123
  (128 shorter events, 73.7 us)
Async XLA Ops:
  0.6 9.7 %copy-start.2 = (f32[8,48,8,128]{3,2,1,0:T(8,128)S(1)}, f32[8,48,8,128]{3,2,1,0:T(8,128)}, u32[]{:S(2)}) copy-start(f32[8,48,8,128]{3,2,1,0:T(8,128)} %param.10) | copy-start | bytes 4718596
  0.7 17.7 %copy-start.22 = (s32[48]{0:T(128)S(1)}, s32[48]{0:T(128)}, u32[]{:S(2)}) copy-start(s32[48]{0:T(128)} %param.12) | copy-start | bytes 580
  0.7 17.7 %copy-start.21 = (f32[48]{0:T(128)S(1)}, f32[48]{0:T(128)}, u32[]{:S(2)}) copy-start(f32[48]{0:T(128)} %param.13) | copy-start | bytes 580
  0.7 17.7 %copy-start.20 = (s32[8,128]{1,0:T(8,128)S(1)}, s32[8,128]{1,0:T(8,128)}, u32[]{:S(2)}) copy-start(s32[8,128]{1,0:T(8,128)} %param.18) | copy-start | bytes 12292
  0.7 17.7 %copy-start.14 = (f32[4,8,128]{2,1,0:T(8,128)S(1)}, f32[4,8,128]{2,1,0:T(8,128)}, u32[]{:S(2)}) copy-start(f32[4,8,128]{2,1,0:T(8,128)} %param.16) | copy-start | bytes 49156
  0.7 18.5 %copy-start.16 = (s32[4,8,128]{2,1,0:T(8,128)S(1)}, s32[4,8,128]{2,1,0:T(8,128)}, u32[]{:S(2)}) copy-start(s32[4,8,128]{2,1,0:T(8,128)} %param.15) | copy-start | bytes 49156
  4.1 17.6 %all-to-all-start = ((bf16[2,137,512]{1,0,2:T(2,128)(2,1)}), bf16[2,137,512]{1,0,2:T(2,128)(2,1)S(1)}, u32[]{:S(2)}, u32[]{:S(2)}) async-start(bf16[2,137,512]{1,0,2:T(2,128)(2,1)} %copy.85), calls=%async_computation | async-start | bytes 1048576 | tf_op jit(solution)/shard_map/all_to_all | solution.py:84
  10.7 60.7 %collective-permute-start.1 = (f32[8,48,3,128]{3,1,2,0:T(8,128)S(1)}, f32[8,48,3,128]{3,1,2,0:T(8,128)}, u32[]{:S(2)}, u32[]{:S(2)}) collective-permute-start(f32[8,48,3,128]{3,1,2,0:T(8,128)S(1)} %copy.94), channel_id=1, source_target_pairs={{4,0},{8,4},{12,8},{16,12},{20,16},{24,20},{28,24},{5,1},{9,5},{13... | collective-permute-start | bytes 1769480 | tf_op jit(solution)/shard_map/ppermute | solution.py:20
  13.1 42.9 %copy-start.19 = (f32[8,48]{1,0:T(8,128)S(1)}, f32[8,48]{1,0:T(8,128)}, u32[]{:S(2)}) copy-start(f32[8,48]{1,0:T(8,128)} %param.19) | copy-start | bytes 4612
  14.0 58.7 %collective-permute-start = (f32[8,48,3,128]{3,1,2,0:T(8,128)}, f32[8,48,3,128]{3,1,2,0:T(8,128)}, u32[]{:S(2)}, u32[]{:S(2)}) collective-permute-start(f32[8,48,3,128]{3,1,2,0:T(8,128)} %copy.93), channel_id=1, source_target_pairs={{0,4},{4,8},{8,12},{12,16},{16,20},{20,24},{24,28},{1,5},{5,9},{9,... | collective-permute-start | bytes 1769480 | tf_op jit(solution)/shard_map/ppermute | solution.py:19
  24.3 24.1 %collective-permute-start.4 = (bf16[97,3,128]{2,1,0:T(4,128)(2,1)S(1)}, bf16[97,3,128]{2,1,0:T(4,128)(2,1)S(1)}, u32[]{:S(2)}, u32[]{:S(2)}) collective-permute-start(bf16[97,3,128]{2,1,0:T(4,128)(2,1)S(1)} %get-tuple-element.46), channel_id=1, source_target_pairs={{0,4},{4,8},{8,12},{12,16},{16,20},{20,24},{24,28},{1,5},{5,9},{9,... | collective-permute-start | bytes 223496 | tf_op jit(solution)/shard_map/ppermute | solution.py:19
  29.0 19.4 %collective-permute-start.5 = (bf16[97,3,128]{2,1,0:T(4,128)(2,1)S(1)}, bf16[97,3,128]{2,1,0:T(4,128)(2,1)S(1)}, u32[]{:S(2)}, u32[]{:S(2)}) collective-permute-start(bf16[97,3,128]{2,1,0:T(4,128)(2,1)S(1)} %get-tuple-element.47), channel_id=1, source_target_pairs={{4,0},{8,4},{12,8},{16,12},{20,16},{24,20},{28,24},{5,1},{9,5},{13... | collective-permute-start | bytes 223496 | tf_op jit(solution)/shard_map/ppermute | solution.py:20
  49.7 9.3 %collective-permute-start.6 = (bf16[97,14,3]{2,1,0:T(8,128)(2,1)}, bf16[97,14,3]{2,1,0:T(8,128)(2,1)S(1)}, u32[]{:S(2)}, u32[]{:S(2)}) collective-permute-start(bf16[97,14,3]{2,1,0:T(8,128)(2,1)} %get-tuple-element.44), channel_id=1, source_target_pairs={{0,1},{1,2},{2,3},{4,5},{5,6},{6,7},{8,9},{9,10},{10,11},{12,13},{... | collective-permute-start | bytes 24452 | tf_op jit(solution)/shard_map/ppermute | solution.py:19
  51.6 9.3 %collective-permute-start.7 = (bf16[97,14,3]{2,1,0:T(8,128)(2,1)}, bf16[97,14,3]{2,1,0:T(8,128)(2,1)S(1)}, u32[]{:S(2)}, u32[]{:S(2)}) collective-permute-start(bf16[97,14,3]{2,1,0:T(8,128)(2,1)} %get-tuple-element.45), channel_id=1, source_target_pairs={{1,0},{2,1},{3,2},{5,4},{6,5},{7,6},{9,8},{10,9},{11,10},{13,12},{... | collective-permute-start | bytes 24452 | tf_op jit(solution)/shard_map/ppermute | solution.py:20
  84.7 14.5 %collective-permute-start.3 = (f32[8,48,14,3]{1,0,3,2:T(8,128)}, f32[8,48,14,3]{1,0,3,2:T(8,128)S(1)}, u32[]{:S(2)}, u32[]{:S(2)}) collective-permute-start(f32[8,48,14,3]{1,0,3,2:T(8,128)} %copy.81), channel_id=1, source_target_pairs={{1,0},{2,1},{3,2},{5,4},{6,5},{7,6},{9,8},{10,9},{11,10},{13,12},{... | collective-permute-start | bytes 193544 | tf_op jit(solution)/shard_map/ppermute | solution.py:20
  88.5 6.9 %collective-permute-start.2 = (f32[8,48,14,3]{1,0,3,2:T(8,128)}, f32[8,48,14,3]{1,0,3,2:T(8,128)S(1)}, u32[]{:S(2)}, u32[]{:S(2)}) collective-permute-start(f32[8,48,14,3]{1,0,3,2:T(8,128)} %copy.80), channel_id=1, source_target_pairs={{0,1},{1,2},{2,3},{4,5},{5,6},{6,7},{8,9},{9,10},{10,11},{12,13},{... | collective-permute-start | bytes 193544 | tf_op jit(solution)/shard_map/ppermute | solution.py:19
  103.0 7.9 %copy-start.15 = (f32[8]{0:T(128)S(1)}, f32[8]{0:T(128)}, u32[]{:S(2)}) copy-start(f32[8]{0:T(128)} %param.17) | copy-start | bytes 100
  139.5 11.1 %copy-start.13 = (f32[8,48]{0,1:T(8,128)S(1)}, f32[8,48]{0,1:T(8,128)}, u32[]{:S(2)}) copy-start(f32[8,48]{0,1:T(8,128)} %copy.88) | copy-start | bytes 4612
  139.5 11.1 %copy-start.17 = (pred[12,132]{1,0:T(8,128)(4,1)S(1)}, pred[12,132]{1,0:T(8,128)(4,1)}, u32[]{:S(2)}) copy-start(pred[12,132]{1,0:T(8,128)(4,1)} %broadcast_and_fusion) | copy-start | bytes 4756
  234.4 8.2 %copy-start.5 = (f32[8,48,8,128]{3,2,0,1:T(8,128)}, f32[8,48,8,128]{3,2,0,1:T(8,128)S(1)}, u32[]{:S(2)}) copy-start(f32[8,48,8,128]{3,2,0,1:T(8,128)S(1)} %slice_multiply_fusion.14) | copy-start | bytes 4718596
  234.4 12.0 %slice-start.2 = ((s8[6291456]{0:T(1024)(128)(4,1)}), s8[4194304]{0:T(1024)(128)(4,1)S(1)}, s32[]{:S(2)}) async-start(s8[6291456]{0:T(1024)(128)(4,1)} %bitcast.66), calls=%async_computation.3 | async-start | bytes 8388608
  234.5 12.0 %slice-start.3 = ((s8[6291456]{0:T(1024)(128)(4,1)}), s8[2097152]{0:T(1024)(128)(4,1)S(1)}, s32[]{:S(2)}) async-start(s8[6291456]{0:T(1024)(128)(4,1)} %bitcast.66), calls=%async_computation.4 | async-start | bytes 4194304
  253.8 8.3 %copy-start.1 = (bf16[2,137,2048]{2,0,1:T(2,128)(2,1)S(1)}, bf16[2,137,2048]{2,0,1:T(2,128)(2,1)}, u32[]{:S(2)}) copy-start(bf16[2,137,2048]{2,0,1:T(2,128)(2,1)} %param.11) | copy-start | bytes 3366916
  253.8 7.6 %copy-start.6 = (f32[8,48,8,128]{3,2,0,1:T(8,128)S(1)}, f32[8,48,8,128]{3,2,0,1:T(8,128)}, u32[]{:S(2)}) copy-start(f32[8,48,8,128]{3,2,0,1:T(8,128)} %copy-done.5) | copy-start | bytes 4718596
  (13 other events, 45.1 us)
where the time goes:
time: 267 us; the launch traced here: 262 us
  other arithmetic  108 us (40%)
  local copies, waits for them, and re-layouts  90.4 us (34%)
  starting transfers between devices  31.3 us (12%)
  waiting for transfers between devices  27.7 us (10%)
  matrix products  3.55 us (1%)
    select_n x3, other arithmetic, per_device(): state = jnp.where(inside[None, None], state, 0.0)  42.5 us
    slice x3, local copies, waits for them, and re-layouts, advance(): div_y = (flux_y[..., 1:, :] - flux_y[..., :-1, :])[..., :, 1:-1]  27.2 us
    slice x3, local copies, waits for them, and re-layouts, advance(): div_x = (flux_x[..., 1:] - flux_x[..., :-1])[..., 1:-1, :]  26 us
    ppermute x4, waiting for transfers between devices, with_halo(): before = lax.ppermute(last, axis, up)  23.4 us
    add x3, other arithmetic, advance(): jnp.maximum(east, 0.0) * padded[..., :, :-1]  21.3 us
    add x3, other arithmetic, advance(): jnp.maximum(north, 0.0) * padded[..., :-1, :]  13.7 us
    ppermute x4, starting transfers between devices, with_halo(): before = lax.ppermute(last, axis, up)  12.8 us
    ppermute x4, starting transfers between devices, with_halo(): after = lax.ppermute(leading, axis, down)  12.3 us
  transfers between devices with their start and end apart: 9, of which 5 were waited for; matrix products, arithmetic and copies ran while one was open for 9% of the time, Pallas kernels for 0%

commit v1 on v0

v1 whole, which is shorter than its diff:
```python
import functools

import jax
import jax.numpy as jnp
from jax import lax
from jax.experimental import pallas as pl
from jax.experimental.pallas import tpu as pltpu
from jax.sharding import PartitionSpec as P

STEPS = 3
KAPPA = 0.05
MESH = pl.DeviceIdType.MESH
UP, DOWN, LEFT, RIGHT = range(4)
BF16 = jnp.bfloat16
F32 = jnp.float32


def kernel(
    n_rows,
    n_cols,
    conc,
    nwp,
    lev_lo,
    frac,
    pick,
    corner_slot,
    corner_wt,
    settle,
    source_mask,
    profile,
    out,
    deposit,
    levels,
    onehot,
    sent,
    got,
    turned,
    norm_wt,
    table_hi,
    table_lo,
    winds,
    wind_row_out,
    wind_row_in,
    wind_col_out,
    wind_col_in,
    row_out,
    row_in,
    col_out,
    col_in,
    edge,
    coef,
    state,
    band_send,
    band_recv,
    wind_send,
    wind_recv,
    halo_send,
    halo_recv,
):
    bins, nz, rd, cd = conc.shape
    ln, columns = nwp.shape[1:]
    cap = pick.shape[3]
    slots = n_rows * cap
    r = lax.axis_index("rows")
    c = lax.axis_index("cols")
    has = (r > 0, r < n_rows - 1, c > 0, c < n_cols - 1)
    target = ({"rows": r - 1}, {"rows": r + 1}, {"cols": c - 1}, {"cols": c + 1})
    lane = lax.broadcasted_iota(jnp.int32, (rd, cd), 1)
    sub = lax.broadcasted_iota(jnp.int32, (rd, cd), 0)
    odd = (lane % 2) == 1
    first_lane, last_lane = lane == 0, lane == cd - 1
    first_sub, last_sub = sub == 0, sub == rd - 1

    barrier = pltpu.get_barrier_semaphore()
    for d in range(1, n_rows):
        pl.semaphore_signal(
            barrier, inc=1, device_id={"rows": lax.rem(r + d, n_rows)}, device_id_type=MESH
        )
    for side in (LEFT, RIGHT):

        @pl.when(has[side])
        def _():
            pl.semaphore_signal(barrier, inc=1, device_id=target[side], device_id_type=MESH)

    for side in (UP, DOWN):

        @pl.when(jnp.logical_not(has[side]))
        def _():
            row_in[:, side] = jnp.zeros(row_in.shape[:1] + row_in.shape[2:], BF16)
            wind_row_in[side] = jnp.zeros(wind_row_in.shape[1:], BF16)

    for side in (LEFT, RIGHT):

        @pl.when(jnp.logical_not(has[side]))
        def _():
            col_in[:, side - 2] = jnp.zeros(col_in.shape[:1] + col_in.shape[2:], F32)
            wind_col_in[side - 2] = jnp.zeros(wind_col_in.shape[1:], F32)

    def pack_group(planes, g):
        acc = jnp.zeros((rd, cd), F32)
        for j, plane in enumerate(planes):
            here = (lane == 2 * j) | (lane == 2 * j + 1)
            acc = jnp.where(here, pltpu.roll(plane, 2 * j + 1, 1), acc)
        return pltpu.roll(acc, 16 * g, 1)

    def unpack(left, right):
        return jnp.where(odd, pltpu.roll(left, 1, 1), pltpu.roll(right, cd - 1, 1))

    def halo_copy(stage, side, b):
        other = side ^ 1
        if side < 2:
            src, dst = row_out.at[stage, side, b], row_in.at[stage, other, b]
        else:
            src, dst = col_out.at[stage, b], col_in.at[stage, other - 2, b]
        return pltpu.make_async_remote_copy(
            src_ref=src,
            dst_ref=dst,
            send_sem=halo_send.at[stage, side, b],
            recv_sem=halo_recv.at[stage, other, b],
            device_id=target[side],
            device_id_type=MESH,
        )

    def halo_arrival(stage, side, b):
        if side < 2:
            src, dst = row_out.at[stage, side, b], row_in.at[stage, side, b]
        else:
            src, dst = col_out.at[stage, b], col_in.at[stage, side - 2, b]
        return pltpu.make_async_remote_copy(
            src_ref=src,
            dst_ref=dst,
            send_sem=halo_send.at[stage, side, b],
            recv_sem=halo_recv.at[stage, side, b],
            device_id=target[side],
            device_id_type=MESH,
        )

    def wind_copy(side):
        other = side ^ 1
        if side < 2:
            src, dst = wind_row_out.at[side], wind_row_in.at[other]
        else:
            src, dst = wind_col_out, wind_col_in.at[other - 2]
        return pltpu.make_async_remote_copy(
            src_ref=src,
            dst_ref=dst,
            send_sem=wind_send.at[side],
            recv_sem=wind_recv.at[other],
            device_id=target[side],
            device_id_type=MESH,
        )

    def wind_arrival(side):
        if side < 2:
            src, dst = wind_row_out.at[side], wind_row_in.at[side]
        else:
            src, dst = wind_col_out, wind_col_in.at[side - 2]
        return pltpu.make_async_remote_copy(
            src_ref=src,
            dst_ref=dst,
            send_sem=wind_send.at[side],
            recv_sem=wind_recv.at[side],
            device_id=target[side],
            device_id_type=MESH,
        )

    def pack_rows(ref, stage, b):
        flat = ref.reshape(bins * nz * rd, cd)
        base = b * (nz * rd)
        row_out[stage, UP, b] = flat[pl.ds(base, nz, stride=rd), :].astype(BF16)
        row_out[stage, DOWN, b] = flat[pl.ds(base + rd - 1, nz, stride=rd), :].astype(BF16)

    def send_halo(stage, b):
        for side in range(4):

            @pl.when(has[side])
            def _():
                halo_copy(stage, side, b).start()

    def first_pack(b, _):
        def group(g, acc):
            return acc + pack_group([conc[b, g * 8 + j] for j in range(8)], g)

        col_out[0, b] = lax.fori_loop(0, nz // 8, group, jnp.zeros((rd, cd), F32))
        pack_rows(conc, 0, b)
        return 0

    lax.fori_loop(0, bins, first_pack, 0)

    pl.semaphore_wait(
        barrier, n_rows - 1 + has[LEFT].astype(jnp.int32) + has[RIGHT].astype(jnp.int32)
    )

    def first_send(b, _):
        send_halo(0, b)
        return 0

    lax.fori_loop(0, bins, first_send, 0)

    diag = lax.broadcasted_iota(jnp.int32, (nz, nz), 0) == lax.broadcasted_iota(
        jnp.int32, (nz, nz), 1
    )
    low = jnp.sum(
        jnp.where(diag, lev_lo[...].astype(F32), 0.0), axis=1, keepdims=True
    ).astype(jnp.int32)
    share = jnp.sum(jnp.where(diag, frac[...], 0.0), axis=1, keepdims=True)
    level_id = lax.broadcasted_iota(jnp.int32, (nz, ln), 1)
    interp = jnp.where(level_id == low, 1.0 - share, 0.0) + jnp.where(
        level_id == low + 1, share, 0.0
    )
    interp_hi = interp.astype(BF16)
    rest = interp - interp_hi.astype(F32)
    interp_mid = rest.astype(BF16)
    interp_lo = (rest - interp_mid.astype(F32)).astype(BF16)
    parts = jnp.concatenate([interp_hi, interp_mid, interp_lo], axis=0)
    for f in range(2):
        mixed = jnp.dot(parts, nwp[f], preferred_element_type=F32)
        levels[f * nz : (f + 1) * nz, :] = (
            mixed[:nz] + mixed[nz : 2 * nz] + mixed[2 * nz :]
        ).astype(BF16)

    def band_copy(source, dest, d):
        return pltpu.make_async_remote_copy(
            src_ref=sent.at[pl.ds(pl.multiple_of(dest * cap, cap), cap)],
            dst_ref=got.at[pl.ds(pl.multiple_of(source * cap, cap), cap)],
            send_sem=band_send.at[d],
            recv_sem=band_recv.at[d],
            device_id={"rows": dest},
            device_id_type=MESH,
        )

    per = 4
    width = per * cap

    def choose(p, _):
        wanted = jnp.concatenate([pick[0, 0, pl.ds(p * per + i, 1), :] for i in range(per)], axis=1)
        step = 128

        def fill(t, _):
            ids = lax.broadcasted_iota(jnp.int32, (step, width), 0) + t * step
            onehot[pl.ds(t * step, step), :] = jnp.where(ids == wanted, 1.0, 0.0).astype(BF16)
            return 0

        lax.fori_loop(0, columns // step, fill, 0)
        chosen = jnp.dot(levels[...], onehot[...], preferred_element_type=F32)
        chosen = jnp.concatenate([chosen, jnp.zeros((128 - 2 * nz, width), F32)], axis=0)
        sent[pl.ds(p * width, width), :] = chosen.T.astype(BF16)
        return 0

    lax.fori_loop(0, n_rows // per, choose, 0)
    for d in range(1, n_rows):
        band_copy(r, lax.rem(r + d, n_rows), d).start()

    weights = corner_wt[...]
    norm_wt[...] = weights / (weights[0] + weights[1] + weights[2] + weights[3])
    chunk = 128

    def fill_table(i, _):
        p = i // (slots // chunk)
        t = i % (slots // chunk)
        ids = lax.broadcasted_iota(jnp.int32, (chunk, cd), 0) + t * chunk
        for half in range(2):
            total = jnp.zeros((chunk, cd), F32)
            for q in range(4):
                slot = corner_slot[q, pl.ds(2 * p + half, 1), :]
                wt = norm_wt[q, pl.ds(2 * p + half, 1), :]
                total = total + jnp.where(ids == slot, wt, 0.0)
            hi = total.astype(BF16)
            where = (p, pl.ds(t * chunk, chunk), pl.ds(half * cd, cd))
            table_hi[where] = hi
            table_lo[where] = (total - hi.astype(F32)).astype(BF16)
        return 0

    lax.fori_loop(0, (rd // 2) * (slots // chunk), fill_table, 0)

    own = pl.ds(pl.multiple_of(r * cap, cap), cap)
    got[own, :] = sent[own, :]
    for d in range(1, n_rows):
        band_copy(lax.rem(r + n_rows - d, n_rows), r, d).wait_recv()
    for t in range(slots // 128):
        turned[:, t * 128 : (t + 1) * 128] = (
            got[t * 128 : (t + 1) * 128, :].astype(F32).T.astype(BF16)
        )
    flat_winds = winds.reshape(2 * nz * rd, cd)
    for p in range(rd // 2):
        blown = jnp.dot(turned[...], table_hi[p], preferred_element_type=F32) + jnp.dot(
            turned[...], table_lo[p], preferred_element_type=F32
        )
        flat_winds[pl.ds(2 * p, 2 * nz, stride=rd), :] = blown[: 2 * nz, :cd]
        flat_winds[pl.ds(2 * p + 1, 2 * nz, stride=rd), :] = blown[: 2 * nz, cd:]

    wind_row_out[UP] = flat_winds[pl.ds(nz * rd, nz, stride=rd), :].astype(BF16)
    wind_row_out[DOWN] = flat_winds[pl.ds(nz * rd + rd - 1, nz, stride=rd), :].astype(BF16)

    def wind_group(g, acc):
        return acc + pack_group([winds[g * 8 + j] for j in range(8)], g)

    wind_col_out[...] = lax.fori_loop(0, nz // 8, wind_group, jnp.zeros((rd, cd), F32))
    for side in range(4):

        @pl.when(has[side])
        def _():
            wind_copy(side).start()

    for side in range(4):

        @pl.when(has[side])
        def _():
            wind_arrival(side).wait_recv()

    def spread_rows(up, down):
        flat = edge.reshape(nz * rd, cd)
        flat[pl.ds(0, nz, stride=rd), :] = up.astype(F32)
        flat[pl.ds(rd - 1, nz, stride=rd), :] = down.astype(F32)

    def across(plane, rim):
        ahead = jnp.where(last_lane, rim, pltpu.roll(plane, cd - 1, 1))
        behind = jnp.where(first_lane, rim, pltpu.roll(plane, 1, 1))
        return ahead, behind

    def along(plane, rim):
        below = jnp.where(last_sub, rim, pltpu.roll(plane, rd - 1, 0))
        above = jnp.where(first_sub, rim, pltpu.roll(plane, 1, 0))
        return below, above

    edge[...] = jnp.zeros_like(edge)
    spread_rows(wind_row_in[UP], wind_row_in[DOWN])
    wind_rim = unpack(wind_col_in[0], wind_col_in[1])

    def coefficients(g, _):
        rims = pltpu.roll(wind_rim, lax.rem(cd - 16 * g, cd), 1)
        for j in range(8):
            k = g * 8 + j
            u, v = winds[k], winds[nz + k]
            u_ahead, u_behind = across(u, pltpu.roll(rims, cd - 2 * j - 1, 1))
            v_below, v_above = along(v, edge[k])
            right, left = 0.5 * (u + u_ahead), 0.5 * (u + u_behind)
            down, up = 0.5 * (v + v_below), 0.5 * (v + v_above)
            coef[0, k] = (
                (1.0 - 4.0 * KAPPA)
                - jnp.maximum(right, 0.0)
                + jnp.minimum(left, 0.0)
                - jnp.maximum(down, 0.0)
                + jnp.minimum(up, 0.0)
            )
            coef[1, k] = KAPPA - jnp.minimum(right, 0.0)
            coef[2, k] = KAPPA + jnp.maximum(left, 0.0)
            coef[3, k] = KAPPA - jnp.minimum(down, 0.0)
            coef[4, k] = KAPPA + jnp.maximum(up, 0.0)
        return 0

    lax.fori_loop(0, nz // 8, coefficients, 0)

    flag = source_mask[...].astype(F32)
    for stage in range(STEPS):
        src = conc if stage == 0 else state
        dst = out if stage == STEPS - 1 else state
        last = stage == STEPS - 1

        def one_bin(b, _):
            for side in range(4):

                @pl.when(has[side])
                def _():
                    halo_arrival(stage, side, b).wait_recv()

            spread_rows(row_in[stage, UP, b], row_in[stage, DOWN, b])
            rim = unpack(col_in[stage, 0, b], col_in[stage, 1, b])
            sink = settle[b]

            def group(g, carry):
                arriving, packed = carry
                rims = pltpu.roll(rim, lax.rem(cd - 16 * g, cd), 1)
                fresh = []
                for j in range(8):
                    k = g * 8 + j
                    a = src[b, k]
                    ahead, behind = across(a, pltpu.roll(rims, cd - 2 * j - 1, 1))
                    below, above = along(a, edge[k])
                    falling = sink * a
                    new = (
                        (coef[0, k] * a + coef[1, k] * ahead)
                        + (coef[2, k] * behind + coef[3, k] * below)
                        + (coef[4, k] * above + flag * profile[b, k])
                        + (arriving - falling)
                    )
                    dst[b, k] = new
                    fresh.append(new)
                    arriving = falling
                if not last:
                    packed = packed + pack_group(fresh, g)
                return arriving, packed

            zero = jnp.zeros((rd, cd), F32)
            fallen, packed = lax.fori_loop(0, nz // 8, group, (zero, zero))
            deposit[b] = fallen if stage == 0 else deposit[b] + fallen
            if not last:
                col_out[stage + 1, b] = packed
                pack_rows(dst, stage + 1, b)
                send_halo(stage + 1, b)
            return 0

        lax.fori_loop(0, bins, one_bin, 0)

    for d in range(1, n_rows):
        band_copy(r, lax.rem(r + d, n_rows), d).wait_send()
    for side in range(4):

        @pl.when(has[side])
        def _():
            wind_copy(side).wait_send()

            def drain(b, _):
                for stage in range(STEPS):
                    halo_copy(stage, side, b).wait_send()
                return 0

            lax.fori_loop(0, bins, drain, 0)


def per_device(conc, nwp, lev_lo, frac, pick, corner_slot, corner_wt, settle, source_mask, profile):
    n_rows, n_cols = lax.axis_size("rows"), lax.axis_size("cols")
    bins, nz, rd, cd = conc.shape
    cap = pick.shape[3]
    slots = n_rows * cap
    columns = nwp.shape[2]
    vmem = pl.BlockSpec(memory_space=pltpu.VMEM)
    smem = pl.BlockSpec(memory_space=pltpu.SMEM)
    return pl.pallas_call(
        functools.partial(kernel, n_rows, n_cols),
        out_shape=(
            jax.ShapeDtypeStruct(conc.shape, F32),
            jax.ShapeDtypeStruct((bins, rd, cd), F32),
        ),
        in_specs=[vmem] * 7 + [smem, vmem, smem],
        out_specs=(vmem, vmem),
        scratch_shapes=[
            pltpu.VMEM((2 * nz, columns), BF16),
            pltpu.VMEM((columns, 4 * cap), BF16),
            pltpu.VMEM((slots, 128), BF16),
            pltpu.VMEM((slots, 128), BF16),
            pltpu.VMEM((128, slots), BF16),
            pltpu.VMEM(corner_wt.shape, F32),
            pltpu.VMEM((rd // 2, slots, 2 * cd), BF16),
            pltpu.VMEM((rd // 2, slots, 2 * cd), BF16),
            pltpu.VMEM((2 * nz, rd, cd), F32),
            pltpu.VMEM((2, nz, cd), BF16),
            pltpu.VMEM((2, nz, cd), BF16),
            pltpu.VMEM((rd, cd), F32),
            pltpu.VMEM((2, rd, cd), F32),
            pltpu.VMEM((STEPS, 2, bins, nz, cd), BF16),
            pltpu.VMEM((STEPS, 2, bins, nz, cd), BF16),
            pltpu.VMEM((STEPS, bins, rd, cd), F32),
            pltpu.VMEM((STEPS, 2, bins, rd, cd), F32),
            pltpu.VMEM((nz, rd, cd), F32),
            pltpu.VMEM((5, nz, rd, cd), F32),
            pltpu.VMEM(conc.shape, F32),
            pltpu.SemaphoreType.DMA((n_rows,)),
            pltpu.SemaphoreType.DMA((n_rows,)),
            pltpu.SemaphoreType.DMA((4,)),
            pltpu.SemaphoreType.DMA((4,)),
            pltpu.SemaphoreType.DMA((STEPS, 4, bins)),
            pltpu.SemaphoreType.DMA((STEPS, 4, bins)),
        ],
        compiler_params=pltpu.CompilerParams(
            collective_id=0, has_side_effects=True, vmem_limit_bytes=48 * 1024 * 1024
        ),
        cost_estimate=pl.CostEstimate(
            flops=10**9, bytes_accessed=6 * 10**6, transcendentals=0
        ),
        name="ash",
    )(
        conc,
        nwp,
        lev_lo.reshape(1, -1),
        frac.reshape(1, -1),
        pick,
        corner_slot,
        corner_wt,
        settle,
        source_mask,
        profile,
    )


def solution(mesh):
    placed = (
        P(None, None, "rows", "cols"),
        P(None, None, "rows"),
        P(),
        P(),
        P("rows", "cols", None, None),
        P(None, "rows", "cols"),
        P(None, "rows", "cols"),
        P(),
        P("rows", "cols"),
        P(),
    )
    return jax.shard_map(
        per_device,
        mesh=mesh,
        in_specs=placed,
        out_specs=(P(None, None, "rows", "cols"), P(None, "rows", "cols")),
        check_vma=False,
    )
```

time: 267 us -> 67.1 us (0.25)
  the two profiles are of different devices: /device:TPU:14 before, /device:TPU:0 now
where the time goes in v1:
time: 67.1 us; the launch traced here: 66.8 us
  Pallas kernels  62.5 us (93%)
  local copies, waits for them, and re-layouts  3.58 us (5%)
  between operations  0.79 us (1%)
    pallas_call x1, Pallas kernels, per_device(): pl.pallas_call(functools.partial(kernel, n_rows, n_cols), out_shape=(jax....  62.5 us
    unnamed x21, local copies, waits for them, and re-layouts  3.58 us

profile of v1, /device:TPU:0, one launch (start us, length us, event | category | flops | bytes accessed | tf_op | source)
XLA Modules:
  0.0 66.8 jit_solution(13582402589093629027)
XLA Ops:
  0.6 0.0 copy-start.5
  0.6 0.0 copy-start.4
  0.7 0.0 copy-start.8
  0.7 0.0 copy-start.2
  0.7 0.0 copy-start.1
  0.7 0.0 copy-start.3
  0.7 0.0 copy-start.7
  0.7 0.0 copy-start.6
  0.7 0.0 copy-start
  0.7 1.8 %copy.12.nwp = bf16[2,137,2048]{2,1,0:T(8,128)(2,1)S(1)} copy(bf16[2,137,2048]{2,0,1:T(2,128)(2,1)} %param.11) | data formatting | bytes 2244608 | tf_op args[1]
  2.5 0.0 copy-done.5
  2.5 0.0 copy-done.4
  2.5 0.0 copy-done.8
  2.5 0.0 copy-done.2
  2.5 0.0 copy-done.1
  2.6 0.0 copy-done.3
  2.6 0.0 copy-done.7
  2.6 0.0 copy-done.6
  2.6 0.0 copy-done
  2.6 62.5 %ash.1 = (f32[8,48,8,128]{3,2,1,0:T(8,128)S(1)}, f32[8,8,128]{2,1,0:T(8,128)S(1)}) custom-call(f32[8,48,8,128]{3,2,1,0:T(8,128)S(1)} %copy-done, bf16[2,137,2048]{2,1,0:T(8,128)(2,1)S(1)} %copy.12.nwp, s32[1,48]{1,0:T(1,128)S(1)} %bitcast.2, f32[1,48]{1,0:T(1,128)S(1)} %bitcast.3, s32[1,1,8,64]{3,2,1,0:T(8,128)S(1)} %copy-done.3, ...), custom_call_target="tpu_custom_call" | custom-call | flops 1000000000 | bytes 6000000 | tf_op jit(solution)/shard_map/ash/pallas_call | solution.py:429
  65.1 1.1 %copy.15 = f32[8,48,8,128]{3,2,1,0:T(8,128)} copy(f32[8,48,8,128]{3,2,1,0:T(8,128)S(1)} %get-tuple-element.4) | data formatting | bytes 3145728
  66.2 0.6 copy.16
Async XLA Ops:
  0.6 1.9 %copy-start.5 = (f32[8,48]{1,0:T(8,128)S(1)}, f32[8,48]{1,0:T(8,128)}, u32[]{:S(2)}) copy-start(f32[8,48]{1,0:T(8,128)} %profile.1) | copy-start | bytes 4612
  0.6 1.9 %copy-start.4 = (s32[8,128]{1,0:T(8,128)S(1)}, s32[8,128]{1,0:T(8,128)}, u32[]{:S(2)}) copy-start(s32[8,128]{1,0:T(8,128)} %source_mask.1) | copy-start | bytes 12292
  0.7 1.9 %copy-start.8 = (f32[8]{0:T(128)S(1)}, f32[8]{0:T(128)}, u32[]{:S(2)}) copy-start(f32[8]{0:T(128)} %settle.1) | copy-start | bytes 100
  0.7 1.9 %copy-start.2 = (f32[4,8,128]{2,1,0:T(8,128)S(1)}, f32[4,8,128]{2,1,0:T(8,128)}, u32[]{:S(2)}) copy-start(f32[4,8,128]{2,1,0:T(8,128)} %corner_wt.1) | copy-start | bytes 49156
  0.7 1.9 %copy-start.1 = (s32[4,8,128]{2,1,0:T(8,128)S(1)}, s32[4,8,128]{2,1,0:T(8,128)}, u32[]{:S(2)}) copy-start(s32[4,8,128]{2,1,0:T(8,128)} %corner_slot.1) | copy-start | bytes 49156
  0.7 1.9 %copy-start.3 = (s32[1,1,8,64]{3,2,1,0:T(8,128)S(1)}, s32[1,1,8,64]{3,2,1,0:T(8,128)}, u32[]{:S(2)}) copy-start(s32[1,1,8,64]{3,2,1,0:T(8,128)} %pick.1) | copy-start | bytes 6148
  0.7 1.9 %copy-start.7 = (f32[48]{0:T(128)S(1)}, f32[48]{0:T(128)}, u32[]{:S(2)}) copy-start(f32[48]{0:T(128)} %param.13) | copy-start | bytes 580
  0.7 1.9 %copy-start.6 = (s32[48]{0:T(128)S(1)}, s32[48]{0:T(128)}, u32[]{:S(2)}) copy-start(s32[48]{0:T(128)} %param.12) | copy-start | bytes 580
  0.7 1.9 %copy-start = (f32[8,48,8,128]{3,2,1,0:T(8,128)S(1)}, f32[8,48,8,128]{3,2,1,0:T(8,128)}, u32[]{:S(2)}) copy-start(f32[8,48,8,128]{3,2,1,0:T(8,128)} %conc.1) | copy-start | bytes 4718596

commit v2 on v1

--- a/solution.py
+++ b/solution.py
@@ -47,9 +47,11 @@
     row_in,
     col_out,
     col_in,
-    edge,
     coef,
-    state,
+    state_a,
+    state_b,
+    spread,
+    flags,
     band_send,
     band_recv,
     wind_send,
@@ -96,12 +98,20 @@
             col_in[:, side - 2] = jnp.zeros(col_in.shape[:1] + col_in.shape[2:], F32)
             wind_col_in[side - 2] = jnp.zeros(wind_col_in.shape[1:], F32)
 
-    def pack_group(planes, g):
-        acc = jnp.zeros((rd, cd), F32)
-        for j, plane in enumerate(planes):
-            here = (lane == 2 * j) | (lane == 2 * j + 1)
-            acc = jnp.where(here, pltpu.roll(plane, 2 * j + 1, 1), acc)
-        return pltpu.roll(acc, 16 * g, 1)
+    groups = nz // rd
+    here = [(lane // 2) == g for g in range(groups)]
+
+    def block(g):
+        return slice(g * rd, (g + 1) * rd)
+
+    def pack(rows):
+        packed = jnp.zeros((rd, cd), F32)
+        for y in range(rd):
+            acc = jnp.zeros((rd, cd), F32)
+            for g in range(groups):
+                acc = jnp.where(here[g], pltpu.roll(rows[y][g], 2 * g + 1, 1), acc)
+            packed = packed + (pltpu.roll(acc, 2 * groups * y, 1) if y else acc)
+        return packed
 
     def unpack(left, right):
         return jnp.where(odd, pltpu.roll(left, 1, 1), pltpu.roll(right, cd - 1, 1))
@@ -164,12 +174,6 @@
             device_id_type=MESH,
         )
 
-    def pack_rows(ref, stage, b):
-        flat = ref.reshape(bins * nz * rd, cd)
-        base = b * (nz * rd)
-        row_out[stage, UP, b] = flat[pl.ds(base, nz, stride=rd), :].astype(BF16)
-        row_out[stage, DOWN, b] = flat[pl.ds(base + rd - 1, nz, stride=rd), :].astype(BF16)
-
     def send_halo(stage, b):
         for side in range(4):
 
@@ -177,25 +181,22 @@
             def _():
                 halo_copy(stage, side, b).start()
 
+    flat_conc = conc.reshape(bins * nz * rd, cd)
+
     def first_pack(b, _):
-        def group(g, acc):
-            return acc + pack_group([conc[b, g * 8 + j] for j in range(8)], g)
-
-        col_out[0, b] = lax.fori_loop(0, nz // 8, group, jnp.zeros((rd, cd), F32))
-        pack_rows(conc, 0, b)
+        rows = []
+        for y in range(rd):
+            row = flat_conc[pl.ds(b * (nz * rd) + y, nz, stride=rd), :]
+            state_a[b, y] = row
+            rows.append([row[block(g)] for g in range(groups)])
+            if y == 0:
+                row_out[0, UP, b] = row.astype(BF16)
+            if y == rd - 1:
+                row_out[0, DOWN, b] = row.astype(BF16)
+        col_out[0, b] = pack(rows)
         return 0
 
     lax.fori_loop(0, bins, first_pack, 0)
-
-    pl.semaphore_wait(
-        barrier, n_rows - 1 + has[LEFT].astype(jnp.int32) + has[RIGHT].astype(jnp.int32)
-    )
-
-    def first_send(b, _):
-        send_halo(0, b)
-        return 0
-
-    lax.fori_loop(0, bins, first_send, 0)
 
     diag = lax.broadcasted_iota(jnp.int32, (nz, nz), 0) == lax.broadcasted_iota(
         jnp.int32, (nz, nz), 1
@@ -248,8 +249,17 @@
         return 0
 
     lax.fori_loop(0, n_rows // per, choose, 0)
+    pl.semaphore_wait(
+        barrier, n_rows - 1 + has[LEFT].astype(jnp.int32) + has[RIGHT].astype(jnp.int32)
+    )
     for d in range(1, n_rows):
         band_copy(r, lax.rem(r + d, n_rows), d).start()
+
+    def first_send(b, _):
+        send_halo(0, b)
+        return 0
+
+    lax.fori_loop(0, bins, first_send, 0)
 
     weights = corner_wt[...]
     norm_wt[...] = weights / (weights[0] + weights[1] + weights[2] + weights[3])
@@ -281,21 +291,16 @@
         turned[:, t * 128 : (t + 1) * 128] = (
             got[t * 128 : (t + 1) * 128, :].astype(F32).T.astype(BF16)
         )
-    flat_winds = winds.reshape(2 * nz * rd, cd)
     for p in range(rd // 2):
         blown = jnp.dot(turned[...], table_hi[p], preferred_element_type=F32) + jnp.dot(
             turned[...], table_lo[p], preferred_element_type=F32
         )
-        flat_winds[pl.ds(2 * p, 2 * nz, stride=rd), :] = blown[: 2 * nz, :cd]
-        flat_winds[pl.ds(2 * p + 1, 2 * nz, stride=rd), :] = blown[: 2 * nz, cd:]
-
-    wind_row_out[UP] = flat_winds[pl.ds(nz * rd, nz, stride=rd), :].astype(BF16)
-    wind_row_out[DOWN] = flat_winds[pl.ds(nz * rd + rd - 1, nz, stride=rd), :].astype(BF16)
-
-    def wind_group(g, acc):
-        return acc + pack_group([winds[g * 8 + j] for j in range(8)], g)
-
-    wind_col_out[...] = lax.fori_loop(0, nz // 8, wind_group, jnp.zeros((rd, cd), F32))
+        winds[2 * p] = blown[: 2 * nz, :cd]
+        winds[2 * p + 1] = blown[: 2 * nz, cd:]
+
+    wind_row_out[UP] = winds[0, nz:, :].astype(BF16)
+    wind_row_out[DOWN] = winds[rd - 1, nz:, :].astype(BF16)
+    wind_col_out[...] = pack([[winds[y, block(g), :] for g in range(groups)] for y in range(rd)])
     for side in range(4):
 
         @pl.when(has[side])
@@ -308,53 +313,49 @@
         def _():
             wind_arrival(side).wait_recv()
 
-    def spread_rows(up, down):
-        flat = edge.reshape(nz * rd, cd)
-        flat[pl.ds(0, nz, stride=rd), :] = up.astype(F32)
-        flat[pl.ds(rd - 1, nz, stride=rd), :] = down.astype(F32)
-
-    def across(plane, rim):
+    def across(plane, rim, y, g):
+        rim = pltpu.roll(rim, cd - 2 * (y * groups + g) - 1, 1)
         ahead = jnp.where(last_lane, rim, pltpu.roll(plane, cd - 1, 1))
         behind = jnp.where(first_lane, rim, pltpu.roll(plane, 1, 1))
         return ahead, behind
 
-    def along(plane, rim):
-        below = jnp.where(last_sub, rim, pltpu.roll(plane, rd - 1, 0))
-        above = jnp.where(first_sub, rim, pltpu.roll(plane, 1, 0))
-        return below, above
-
-    edge[...] = jnp.zeros_like(edge)
-    spread_rows(wind_row_in[UP], wind_row_in[DOWN])
     wind_rim = unpack(wind_col_in[0], wind_col_in[1])
-
-    def coefficients(g, _):
-        rims = pltpu.roll(wind_rim, lax.rem(cd - 16 * g, cd), 1)
-        for j in range(8):
-            k = g * 8 + j
-            u, v = winds[k], winds[nz + k]
-            u_ahead, u_behind = across(u, pltpu.roll(rims, cd - 2 * j - 1, 1))
-            v_below, v_above = along(v, edge[k])
+    wind_rows = (
+        [wind_row_in[UP].astype(F32)]
+        + [winds[y, nz:, :] for y in range(rd)]
+        + [wind_row_in[DOWN].astype(F32)]
+    )
+    for y in range(rd):
+        for g in range(groups):
+            k = block(g)
+            u = winds[y, k, :]
+            u_ahead, u_behind = across(u, wind_rim, y, g)
+            v_above, v, v_below = (wind_rows[y + i][k] for i in range(3))
             right, left = 0.5 * (u + u_ahead), 0.5 * (u + u_behind)
             down, up = 0.5 * (v + v_below), 0.5 * (v + v_above)
-            coef[0, k] = (
+            coef[0, y, k, :] = (
                 (1.0 - 4.0 * KAPPA)
                 - jnp.maximum(right, 0.0)
                 + jnp.minimum(left, 0.0)
                 - jnp.maximum(down, 0.0)
                 + jnp.minimum(up, 0.0)
             )
-            coef[1, k] = KAPPA - jnp.minimum(right, 0.0)
-            coef[2, k] = KAPPA + jnp.maximum(left, 0.0)
-            coef[3, k] = KAPPA - jnp.minimum(down, 0.0)
-            coef[4, k] = KAPPA + jnp.maximum(up, 0.0)
-        return 0
-
-    lax.fori_loop(0, nz // 8, coefficients, 0)
-
-    flag = source_mask[...].astype(F32)
+            coef[1, y, k, :] = KAPPA - jnp.minimum(right, 0.0)
+            coef[2, y, k, :] = KAPPA + jnp.maximum(left, 0.0)
+            coef[3, y, k, :] = KAPPA - jnp.minimum(down, 0.0)
+            coef[4, y, k, :] = KAPPA + jnp.maximum(up, 0.0)
+
+    diag = lax.broadcasted_iota(jnp.int32, (nz, nz), 0) == lax.broadcasted_iota(
+        jnp.int32, (nz, nz), 1
+    )
+    for b in range(bins):
+        column = jnp.sum(jnp.where(diag, profile[b : b + 1, :], 0.0), axis=1, keepdims=True)
+        spread[b] = jnp.broadcast_to(column, (nz, cd))
+    flags[...] = source_mask[...].astype(F32)
+    flat_out = out.reshape(bins * nz * rd, cd)
     for stage in range(STEPS):
-        src = conc if stage == 0 else state
-        dst = out if stage == STEPS - 1 else state
+        src = (state_a, state_b)[stage % 2]
+        dst = (state_b, state_a)[stage % 2]
         last = stage == STEPS - 1
 
         def one_bin(b, _):
@@ -364,39 +365,46 @@
                 def _():
                     halo_arrival(stage, side, b).wait_recv()
 
-            spread_rows(row_in[stage, UP, b], row_in[stage, DOWN, b])
             rim = unpack(col_in[stage, 0, b], col_in[stage, 1, b])
             sink = settle[b]
-
-            def group(g, carry):
-                arriving, packed = carry
-                rims = pltpu.roll(rim, lax.rem(cd - 16 * g, cd), 1)
-                fresh = []
-                for j in range(8):
-                    k = g * 8 + j
-                    a = src[b, k]
-                    ahead, behind = across(a, pltpu.roll(rims, cd - 2 * j - 1, 1))
-                    below, above = along(a, edge[k])
+            rows = (
+                [row_in[stage, UP, b].astype(F32)]
+                + [src[b, y] for y in range(rd)]
+                + [row_in[stage, DOWN, b].astype(F32)]
+            )
+            fresh = []
+            for y in range(rd):
+                flag = flags[y : y + 1, :]
+                news = []
+                turned_over = jnp.zeros((rd, cd), F32)
+                for g in range(groups):
+                    k = block(g)
+                    above, a, below = (rows[y + i][k] for i in range(3))
+                    ahead, behind = across(a, rim, y, g)
                     falling = sink * a
+                    rolled = pltpu.roll(falling, 1, 0)
+                    arriving = jnp.where(first_sub, turned_over, rolled)
+                    turned_over = rolled
                     new = (
-                        (coef[0, k] * a + coef[1, k] * ahead)
-                        + (coef[2, k] * behind + coef[3, k] * below)
-                        + (coef[4, k] * above + flag * profile[b, k])
+                        (coef[0, y, k, :] * a + coef[1, y, k, :] * ahead)
+                        + (coef[2, y, k, :] * behind + coef[3, y, k, :] * below)
+                        + (coef[4, y, k, :] * above + flag * spread[b, k, :])
                         + (arriving - falling)
                     )
-                    dst[b, k] = new
-                    fresh.append(new)
-                    arriving = falling
-                if not last:
-                    packed = packed + pack_group(fresh, g)
-                return arriving, packed
-
-            zero = jnp.zeros((rd, cd), F32)
-            fallen, packed = lax.fori_loop(0, nz // 8, group, (zero, zero))
-            deposit[b] = fallen if stage == 0 else deposit[b] + fallen
+                    if last:
+                        flat_out[pl.ds(b * (nz * rd) + g * (rd * rd) + y, rd, stride=rd), :] = new
+                    else:
+                        dst[b, y, k, :] = new
+                    news.append(new)
+                fallen = falling[rd - 1 :, :]
+                here_row = (b, slice(y, y + 1), slice(None))
+                deposit[here_row] = fallen if stage == 0 else deposit[here_row] + fallen
+                fresh.append(news)
+                if not last and y == 0:
+                    row_out[stage + 1, UP, b] = jnp.concatenate(news, axis=0).astype(BF16)
             if not last:
-                col_out[stage + 1, b] = packed
-                pack_rows(dst, stage + 1, b)
+                row_out[stage + 1, DOWN, b] = jnp.concatenate(fresh[-1], axis=0).astype(BF16)
+                col_out[stage + 1, b] = pack(fresh)
                 send_halo(stage + 1, b)
             return 0
 
@@ -432,7 +440,7 @@
             jax.ShapeDtypeStruct(conc.shape, F32),
             jax.ShapeDtypeStruct((bins, rd, cd), F32),
         ),
-        in_specs=[vmem] * 7 + [smem, vmem, smem],
+        in_specs=[vmem] * 7 + [smem, vmem, vmem],
         out_specs=(vmem, vmem),
         scratch_shapes=[
             pltpu.VMEM((2 * nz, columns), BF16),
@@ -443,7 +451,7 @@
             pltpu.VMEM(corner_wt.shape, F32),
             pltpu.VMEM((rd // 2, slots, 2 * cd), BF16),
             pltpu.VMEM((rd // 2, slots, 2 * cd), BF16),
-            pltpu.VMEM((2 * nz, rd, cd), F32),
+            pltpu.VMEM((rd, 2 * nz, cd), F32),
             pltpu.VMEM((2, nz, cd), BF16),
             pltpu.VMEM((2, nz, cd), BF16),
             pltpu.VMEM((rd, cd), F32),
@@ -452,9 +460,11 @@
             pltpu.VMEM((STEPS, 2, bins, nz, cd), BF16),
             pltpu.VMEM((STEPS, bins, rd, cd), F32),
             pltpu.VMEM((STEPS, 2, bins, rd, cd), F32),
-            pltpu.VMEM((nz, rd, cd), F32),
-            pltpu.VMEM((5, nz, rd, cd), F32),
-            pltpu.VMEM(conc.shape, F32),
+            pltpu.VMEM((5, rd, nz, cd), F32),
+            pltpu.VMEM((bins, rd, nz, cd), F32),
+            pltpu.VMEM((bins, rd, nz, cd), F32),
+            pltpu.VMEM((bins, nz, cd), F32),
+            pltpu.VMEM((rd, cd), F32),
             pltpu.SemaphoreType.DMA((n_rows,)),
             pltpu.SemaphoreType.DMA((n_rows,)),
             pltpu.SemaphoreType.DMA((4,)),

time: 67.1 us -> 33.2 us (0.49)
  Pallas kernels: 62.5 us -> 28.7 us
    pallas_call x1, Pallas kernels: 62.5 us -> 28.7 us  [per_device(): pl.pallas_call(functools.partial(kernel, n_rows, n_cols), out_shape=(jax....]
where the time goes in v2:
time: 33.2 us; the launch traced here: 33.1 us
  Pallas kernels  28.7 us (86%)
  local copies, waits for them, and re-layouts  3.58 us (11%)
  between operations  0.79 us (2%)
    pallas_call x1, Pallas kernels, per_device(): pl.pallas_call(functools.partial(kernel, n_rows, n_cols), out_shape=(jax....  28.7 us
    unnamed x21, local copies, waits for them, and re-layouts  3.58 us

profile of v2, /device:TPU:0, one launch (start us, length us, event | category | flops | bytes accessed | tf_op | source)
XLA Modules:
  0.0 33.1 jit_solution(13046658986162301795)
XLA Ops:
  0.6 0.0 copy-start.5
  0.6 0.0 copy-start.4
  0.7 0.0 copy-start.8
  0.7 0.0 copy-start.2
  0.7 0.0 copy-start.1
  0.7 0.0 copy-start.3
  0.7 0.0 copy-start.7
  0.7 0.0 copy-start.6
  0.7 0.0 copy-start
  0.7 1.8 %copy.12.nwp = bf16[2,137,2048]{2,1,0:T(8,128)(2,1)S(1)} copy(bf16[2,137,2048]{2,0,1:T(2,128)(2,1)} %param.11) | data formatting | bytes 2244608 | tf_op args[1]
  2.5 0.0 copy-done.5
  2.5 0.0 copy-done.4
  2.5 0.0 copy-done.8
  2.5 0.0 copy-done.2
  2.5 0.0 copy-done.1
  2.6 0.0 copy-done.3
  2.6 0.0 copy-done.7
  2.6 0.0 copy-done.6
  2.6 0.0 copy-done
  2.6 28.7 %ash.1 = (f32[8,48,8,128]{3,2,1,0:T(8,128)S(1)}, f32[8,8,128]{2,1,0:T(8,128)S(1)}) custom-call(f32[8,48,8,128]{3,2,1,0:T(8,128)S(1)} %copy-done, bf16[2,137,2048]{2,1,0:T(8,128)(2,1)S(1)} %copy.12.nwp, s32[1,48]{1,0:T(1,128)S(1)} %bitcast.2, f32[1,48]{1,0:T(1,128)S(1)} %bitcast.3, s32[1,1,8,64]{3,2,1,0:T(8,128)S(1)} %copy-done.3, ...), custom_call_target="tpu_custom_call" | custom-call | flops 1000000000 | bytes 6000000 | tf_op jit(solution)/shard_map/ash/pallas_call | solution.py:437
  31.3 1.1 %copy.15 = f32[8,48,8,128]{3,2,1,0:T(8,128)} copy(f32[8,48,8,128]{3,2,1,0:T(8,128)S(1)} %get-tuple-element.4) | data formatting | bytes 3145728
  32.5 0.6 %copy.16 = f32[8,8,128]{2,1,0:T(8,128)} copy(f32[8,8,128]{2,1,0:T(8,128)S(1)} %get-tuple-element.5) | data formatting | bytes 65536
Async XLA Ops:
  0.6 1.9 %copy-start.5 = (f32[8,48]{1,0:T(8,128)S(1)}, f32[8,48]{1,0:T(8,128)}, u32[]{:S(2)}) copy-start(f32[8,48]{1,0:T(8,128)} %profile.1) | copy-start | bytes 4612
  0.6 1.9 %copy-start.4 = (s32[8,128]{1,0:T(8,128)S(1)}, s32[8,128]{1,0:T(8,128)}, u32[]{:S(2)}) copy-start(s32[8,128]{1,0:T(8,128)} %source_mask.1) | copy-start | bytes 12292
  0.7 1.9 %copy-start.8 = (f32[8]{0:T(128)S(1)}, f32[8]{0:T(128)}, u32[]{:S(2)}) copy-start(f32[8]{0:T(128)} %settle.1) | copy-start | bytes 100
  0.7 1.9 %copy-start.2 = (f32[4,8,128]{2,1,0:T(8,128)S(1)}, f32[4,8,128]{2,1,0:T(8,128)}, u32[]{:S(2)}) copy-start(f32[4,8,128]{2,1,0:T(8,128)} %corner_wt.1) | copy-start | bytes 49156
  0.7 1.9 %copy-start.1 = (s32[4,8,128]{2,1,0:T(8,128)S(1)}, s32[4,8,128]{2,1,0:T(8,128)}, u32[]{:S(2)}) copy-start(s32[4,8,128]{2,1,0:T(8,128)} %corner_slot.1) | copy-start | bytes 49156
  0.7 1.9 %copy-start.3 = (s32[1,1,8,64]{3,2,1,0:T(8,128)S(1)}, s32[1,1,8,64]{3,2,1,0:T(8,128)}, u32[]{:S(2)}) copy-start(s32[1,1,8,64]{3,2,1,0:T(8,128)} %pick.1) | copy-start | bytes 6148
  0.7 1.9 %copy-start.7 = (f32[48]{0:T(128)S(1)}, f32[48]{0:T(128)}, u32[]{:S(2)}) copy-start(f32[48]{0:T(128)} %param.13) | copy-start | bytes 580
  0.7 1.9 %copy-start.6 = (s32[48]{0:T(128)S(1)}, s32[48]{0:T(128)}, u32[]{:S(2)}) copy-start(s32[48]{0:T(128)} %param.12) | copy-start | bytes 580
  0.7 1.9 %copy-start = (f32[8,48,8,128]{3,2,1,0:T(8,128)S(1)}, f32[8,48,8,128]{3,2,1,0:T(8,128)}, u32[]{:S(2)}) copy-start(f32[8,48,8,128]{3,2,1,0:T(8,128)} %conc.1) | copy-start | bytes 4718596

commit v3 on v2

v3 whole, which is shorter than its diff:
```python
import functools

import jax
import jax.numpy as jnp
from jax import lax
from jax.experimental import pallas as pl
from jax.experimental.pallas import tpu as pltpu
from jax.sharding import PartitionSpec as P

STEPS = 3
KAPPA = 0.05
MESH = pl.DeviceIdType.MESH
UP, DOWN, LEFT, RIGHT = range(4)
BF16 = jnp.bfloat16
F32 = jnp.float32


def kernel(
    n_rows,
    n_cols,
    conc,
    nwp,
    lev_lo,
    frac,
    pick,
    corner_slot,
    corner_wt,
    settle,
    source_mask,
    profile,
    out,
    deposit,
    levels,
    onehot,
    sent,
    got,
    turned,
    norm_wt,
    table_hi,
    table_lo,
    winds,
    wind_row_out,
    wind_row_in,
    wind_col_out,
    wind_col_in,
    wind_diag_in,
    flag_out,
    flag_in,
    row_out,
    row_in,
    col_out,
    col_in,
    coef,
    state_a,
    state_b,
    spread,
    flags,
    band_send,
    band_recv,
    wind_send,
    wind_recv,
    diag_send,
    diag_recv,
    flag_send,
    flag_recv,
    row_send,
    row_recv,
    col_send,
    col_recv,
):
    bins, nz, rd, cd = conc.shape
    ln, columns = nwp.shape[1:]
    cap = pick.shape[3]
    slots = n_rows * cap
    r = lax.axis_index("rows")
    c = lax.axis_index("cols")
    has = (r > 0, r < n_rows - 1, c > 0, c < n_cols - 1)
    target = ({"rows": r - 1}, {"rows": r + 1}, {"cols": c - 1}, {"cols": c + 1})
    lane = lax.broadcasted_iota(jnp.int32, (rd, cd), 1)
    sub = lax.broadcasted_iota(jnp.int32, (rd, cd), 0)
    odd = (lane % 2) == 1
    first_lane, last_lane = lane == 0, lane == cd - 1
    first_sub = sub == 0
    corners = [(v, h) for v in (UP, DOWN) for h in (LEFT, RIGHT)]
    has_corner = [has[v] & has[h] for v, h in corners]
    to_corner = [{**target[v], **target[h]} for v, h in corners]

    barrier = pltpu.get_barrier_semaphore()
    for d in range(1, n_rows):
        pl.semaphore_signal(
            barrier, inc=1, device_id={"rows": lax.rem(r + d, n_rows)}, device_id_type=MESH
        )
    for side in (LEFT, RIGHT):

        @pl.when(has[side])
        def _():
            pl.semaphore_signal(barrier, inc=1, device_id=target[side], device_id_type=MESH)

    for i in range(4):

        @pl.when(has_corner[i])
        def _():
            pl.semaphore_signal(barrier, inc=1, device_id=to_corner[i], device_id_type=MESH)

    for side in (UP, DOWN):

        @pl.when(jnp.logical_not(has[side]))
        def _():
            row_in[side] = jnp.zeros(row_in.shape[1:], BF16)
            wind_row_in[side] = jnp.zeros(wind_row_in.shape[1:], BF16)
            flag_in[side] = jnp.zeros(flag_in.shape[1:], BF16)

    for side in (LEFT, RIGHT):

        @pl.when(jnp.logical_not(has[side]))
        def _():
            col_in[side - 2] = jnp.zeros(col_in.shape[1:], F32)
            wind_col_in[side - 2] = jnp.zeros(wind_col_in.shape[1:], F32)

    for i in range(4):

        @pl.when(jnp.logical_not(has_corner[i]))
        def _():
            wind_diag_in[i] = jnp.zeros((rd, cd), F32)

    groups = nz // rd
    here = [(lane // 2) == g for g in range(groups)]

    def block(g):
        return slice(g * rd, (g + 1) * rd)

    def pack(rows):
        packed = jnp.zeros((rd, cd), F32)
        for i, row in rows:
            acc = jnp.zeros((rd, cd), F32)
            for g in range(groups):
                acc = jnp.where(here[g], pltpu.roll(row[g], 2 * g + 1, 1), acc)
            packed = packed + (pltpu.roll(acc, 2 * groups * i, 1) if i else acc)
        return packed

    def split(row):
        return [row[block(g)] for g in range(groups)]

    def unpack(left, right):
        return jnp.where(odd, pltpu.roll(left, 1, 1), pltpu.roll(right, cd - 1, 1))

    def push(side, src, dst, send_sem, recv_sem):
        return pltpu.make_async_remote_copy(
            src_ref=src,
            dst_ref=dst,
            send_sem=send_sem,
            recv_sem=recv_sem,
            device_id=target[side],
            device_id_type=MESH,
        )

    def row_copy(side, b, arrival=False):
        end = side if arrival else side ^ 1
        return push(
            side, row_out.at[side, b], row_in.at[end, b], row_send.at[side, b], row_recv.at[end, b]
        )

    def col_copy(kind, side, b, arrival=False):
        end = (side if arrival else side ^ 1) - 2
        return push(
            side,
            col_out.at[kind, b],
            col_in.at[end, kind, b],
            col_send.at[kind, side - 2, b],
            col_recv.at[kind, end, b],
        )

    def flag_copy(side, arrival=False):
        end = side if arrival else side ^ 1
        return push(side, flag_out, flag_in.at[end], flag_send.at[side], flag_recv.at[end])

    def wind_copy(side, arrival=False):
        end = side if arrival else side ^ 1
        if side < 2:
            src, dst = wind_row_out.at[side], wind_row_in.at[end]
        else:
            src, dst = wind_col_out, wind_col_in.at[end - 2]
        return push(side, src, dst, wind_send.at[side], wind_recv.at[end])

    def diag_copy(i, arrival=False):
        end = i if arrival else 3 - i
        return pltpu.make_async_remote_copy(
            src_ref=wind_col_out,
            dst_ref=wind_diag_in.at[end],
            send_sem=diag_send.at[i],
            recv_sem=diag_recv.at[end],
            device_id=to_corner[i],
            device_id_type=MESH,
        )

    def each(sides, act):
        for side in sides:

            @pl.when(has[side])
            def _():
                act(side)

    def send_rows(first, end):
        def one(b, _):
            each((UP, DOWN), lambda side: row_copy(side, b).start())
            return 0

        lax.fori_loop(first, end, one, 0)

    def send_cols(kind, b):
        each((LEFT, RIGHT), lambda side: col_copy(kind, side, b).start())

    flat_conc = conc.reshape(bins * nz * rd, cd)
    margin = STEPS
    reach = margin - 1

    def first_pack(b, _):
        rows = []
        for y in range(rd):
            row = flat_conc[pl.ds(b * (nz * rd) + y, nz, stride=rd), :]
            state_a[b, y + reach] = row
            rows.append((y, split(row)))
            if y < margin:
                row_out[UP, b, y * nz : (y + 1) * nz, :] = row.astype(BF16)
            if rd - 1 - y < margin:
                i = rd - 1 - y
                row_out[DOWN, b, i * nz : (i + 1) * nz, :] = row.astype(BF16)
        col_out[0, b] = pack(rows)
        return 0

    lax.fori_loop(0, bins, first_pack, 0)
    mask = source_mask[...].astype(F32)
    flags[reach : reach + rd, :] = mask
    flag_out[...] = jnp.concatenate([mask, jnp.zeros_like(mask)], axis=0).astype(BF16)

    def count(flag):
        return flag.astype(jnp.int32)

    pl.semaphore_wait(
        barrier,
        n_rows - 1 + count(has[LEFT]) + count(has[RIGHT]) + sum(count(h) for h in has_corner),
    )
    early, middle = (3 * bins) // 8, (6 * bins) // 8
    each((UP, DOWN), lambda side: flag_copy(side).start())
    send_rows(0, early)

    def first_cols(b, _):
        send_cols(0, b)
        return 0

    lax.fori_loop(0, bins, first_cols, 0)

    diag = lax.broadcasted_iota(jnp.int32, (nz, nz), 0) == lax.broadcasted_iota(
        jnp.int32, (nz, nz), 1
    )
    low = jnp.sum(
        jnp.where(diag, lev_lo[...].astype(F32), 0.0), axis=1, keepdims=True
    ).astype(jnp.int32)
    share = jnp.sum(jnp.where(diag, frac[...], 0.0), axis=1, keepdims=True)
    level_id = lax.broadcasted_iota(jnp.int32, (nz, ln), 1)
    interp = jnp.where(level_id == low, 1.0 - share, 0.0) + jnp.where(
        level_id == low + 1, share, 0.0
    )
    interp_hi = interp.astype(BF16)
    rest = interp - interp_hi.astype(F32)
    interp_mid = rest.astype(BF16)
    interp_lo = (rest - interp_mid.astype(F32)).astype(BF16)
    parts = jnp.concatenate([interp_hi, interp_mid, interp_lo], axis=0)
    for f in range(2):
        mixed = jnp.dot(parts, nwp[f], preferred_element_type=F32)
        levels[f * nz : (f + 1) * nz, :] = (
            mixed[:nz] + mixed[nz : 2 * nz] + mixed[2 * nz :]
        ).astype(BF16)

    def band_copy(source, dest, d):
        return pltpu.make_async_remote_copy(
            src_ref=sent.at[pl.ds(pl.multiple_of(dest * cap, cap), cap)],
            dst_ref=got.at[pl.ds(pl.multiple_of(source * cap, cap), cap)],
            send_sem=band_send.at[d],
            recv_sem=band_recv.at[d],
            device_id={"rows": dest},
            device_id_type=MESH,
        )

    per = 4
    width = per * cap

    def choose(p, _):
        wanted = jnp.concatenate([pick[0, 0, pl.ds(p * per + i, 1), :] for i in range(per)], axis=1)
        step = 128

        def fill(t, _):
            ids = lax.broadcasted_iota(jnp.int32, (step, width), 0) + t * step
            onehot[pl.ds(t * step, step), :] = jnp.where(ids == wanted, 1.0, 0.0).astype(BF16)
            return 0

        lax.fori_loop(0, columns // step, fill, 0)
        chosen = jnp.dot(levels[...], onehot[...], preferred_element_type=F32)
        chosen = jnp.concatenate([chosen, jnp.zeros((128 - 2 * nz, width), F32)], axis=0)
        sent[pl.ds(p * width, width), :] = chosen.T.astype(BF16)
        return 0

    lax.fori_loop(0, n_rows // per, choose, 0)
    for d in range(1, n_rows):
        band_copy(r, lax.rem(r + d, n_rows), d).start()

    send_rows(early, middle)

    weights = corner_wt[...]
    norm_wt[...] = weights / (weights[0] + weights[1] + weights[2] + weights[3])
    chunk = 128

    def fill_table(i, _):
        p = i // (slots // chunk)
        t = i % (slots // chunk)
        ids = lax.broadcasted_iota(jnp.int32, (chunk, cd), 0) + t * chunk
        for half in range(2):
            total = jnp.zeros((chunk, cd), F32)
            for q in range(4):
                slot = corner_slot[q, pl.ds(2 * p + half, 1), :]
                wt = norm_wt[q, pl.ds(2 * p + half, 1), :]
                total = total + jnp.where(ids == slot, wt, 0.0)
            hi = total.astype(BF16)
            where = (p, pl.ds(t * chunk, chunk), pl.ds(half * cd, cd))
            table_hi[where] = hi
            table_lo[where] = (total - hi.astype(F32)).astype(BF16)
        return 0

    lax.fori_loop(0, (rd // 2) * (slots // chunk), fill_table, 0)

    diag = lax.broadcasted_iota(jnp.int32, (nz, nz), 0) == lax.broadcasted_iota(
        jnp.int32, (nz, nz), 1
    )
    for b in range(bins):
        column = jnp.sum(jnp.where(diag, profile[b : b + 1, :], 0.0), axis=1, keepdims=True)
        spread[b] = jnp.broadcast_to(column, (nz, cd))

    own = pl.ds(pl.multiple_of(r * cap, cap), cap)
    got[own, :] = sent[own, :]
    for d in range(1, n_rows):
        band_copy(lax.rem(r + n_rows - d, n_rows), r, d).wait_recv()
    for t in range(slots // 128):
        turned[:, t * 128 : (t + 1) * 128] = (
            got[t * 128 : (t + 1) * 128, :].astype(F32).T.astype(BF16)
        )
    for p in range(rd // 2):
        blown = jnp.dot(turned[...], table_hi[p], preferred_element_type=F32) + jnp.dot(
            turned[...], table_lo[p], preferred_element_type=F32
        )
        winds[2 * p] = blown[: 2 * nz, :cd]
        winds[2 * p + 1] = blown[: 2 * nz, cd:]

    for side, order in ((UP, range(reach + 1)), (DOWN, range(rd - 1, rd - 2 - reach, -1))):
        for i, y in enumerate(order):
            kept = winds[y] if i < reach else winds[y, nz:, :]
            wind_row_out[side, 2 * i * nz : 2 * i * nz + kept.shape[0], :] = kept.astype(BF16)
    wind_col_out[...] = pack(
        [(y, [winds[y, block(g), :] for g in range(groups)]) for y in range(rd)]
    )
    each(range(4), lambda side: wind_copy(side).start())
    for i in range(4):

        @pl.when(has_corner[i])
        def _():
            diag_copy(i).start()

    send_rows(middle, bins)

    def outer_cols(b):
        each((UP, DOWN), lambda side: row_copy(side, b, arrival=True).wait_recv())
        rows = []
        for i in range(reach):
            k = slice(i * nz, (i + 1) * nz)
            rows.append((reach - 1 - i, split(row_in[UP, b, k, :].astype(F32))))
            rows.append((reach + i, split(row_in[DOWN, b, k, :].astype(F32))))
        col_out[1, b] = pack(rows)
        send_cols(1, b)

    ahead_of = min(3, bins)

    def first_outer(b, _):
        outer_cols(b)
        return 0

    lax.fori_loop(0, ahead_of, first_outer, 0)
    each((UP, DOWN), lambda side: flag_copy(side, arrival=True).wait_recv())
    flags[:reach, :] = flag_in[UP].astype(F32)[rd - reach : rd]
    flags[reach + rd : reach + rd + reach, :] = flag_in[DOWN].astype(F32)[:reach]
    each(range(4), lambda side: wind_copy(side, arrival=True).wait_recv())
    for i in range(4):

        @pl.when(has_corner[i])
        def _():
            diag_copy(i, arrival=True).wait_recv()

    def across(plane, rim, i, g):
        rim = pltpu.roll(rim, cd - 2 * (i * groups + g) - 1, 1)
        ahead = jnp.where(last_lane, rim, pltpu.roll(plane, cd - 1, 1))
        behind = jnp.where(first_lane, rim, pltpu.roll(plane, 1, 1))
        return ahead, behind

    def outer_wind(side, i, f):
        return wind_row_in[side, (2 * i + f) * nz : (2 * i + f + 1) * nz, :].astype(F32)

    last_row = [
        wind_row_in[side, 2 * reach * nz : (2 * reach + 1) * nz, :].astype(F32)
        for side in (UP, DOWN)
    ]
    easts = (
        [outer_wind(UP, i, 0) for i in reversed(range(reach))]
        + [winds[y, :nz, :] for y in range(rd)]
        + [outer_wind(DOWN, i, 0) for i in range(reach)]
    )
    norths = (
        [last_row[0]]
        + [outer_wind(UP, i, 1) for i in reversed(range(reach))]
        + [winds[y, nz:, :] for y in range(rd)]
        + [outer_wind(DOWN, i, 1) for i in range(reach)]
        + [last_row[1]]
    )
    wind_rim = unpack(wind_col_in[0], wind_col_in[1])
    upper_rim = unpack(wind_diag_in[0], wind_diag_in[1])
    lower_rim = unpack(wind_diag_in[2], wind_diag_in[3])
    for y in range(-reach, rd + reach):
        at = y + reach
        rim, i = (
            (upper_rim, y + rd) if y < 0 else (wind_rim, y) if y < rd else (lower_rim, y - rd)
        )
        for g in range(groups):
            k = block(g)
            u = easts[at][k]
            u_ahead, u_behind = across(u, rim, i, g)
            v_above, v, v_below = (norths[at + i][k] for i in range(3))
            right, left = 0.5 * (u + u_ahead), 0.5 * (u + u_behind)
            down, up = 0.5 * (v + v_below), 0.5 * (v + v_above)
            coef[0, at, k, :] = (
                (1.0 - 4.0 * KAPPA)
                - jnp.maximum(right, 0.0)
                + jnp.minimum(left, 0.0)
                - jnp.maximum(down, 0.0)
                + jnp.minimum(up, 0.0)
            )
            coef[1, at, k, :] = KAPPA - jnp.minimum(right, 0.0)
            coef[2, at, k, :] = KAPPA + jnp.maximum(left, 0.0)
            coef[3, at, k, :] = KAPPA - jnp.minimum(down, 0.0)
            coef[4, at, k, :] = KAPPA + jnp.maximum(up, 0.0)

    keep = [has[UP].astype(F32), has[DOWN].astype(F32)]
    flat_out = out.reshape(bins * nz * rd, cd)
    for stage in range(STEPS):
        src = (state_a, state_b)[stage % 2]
        dst = (state_b, state_a)[stage % 2]
        last = stage == STEPS - 1

        def one_bin(b, _):
            if stage == 0:

                @pl.when(b + ahead_of < bins)
                def _():
                    outer_cols(b + ahead_of)

            kinds = (2 * stage,) if last else (2 * stage, 2 * stage + 1)
            for kind in kinds:
                each((LEFT, RIGHT), lambda side: col_copy(kind, side, b, arrival=True).wait_recv())
            rims = [unpack(col_in[0, kind, b], col_in[1, kind, b]) for kind in kinds]
            sink = settle[b]
            grow = reach - stage

            def source(y):
                if stage == 0 and y < 0:
                    return row_in[UP, b, (-1 - y) * nz : -y * nz, :].astype(F32)
                if stage == 0 and y >= rd:
                    return row_in[DOWN, b, (y - rd) * nz : (y - rd + 1) * nz, :].astype(F32)
                return src[b, y + reach]

            rows = [source(y) for y in range(-grow - 1, rd + grow + 1)]
            fresh = []
            outer = []
            for y in range(-grow, rd + grow):
                main = 0 <= y < rd
                at = y + reach
                flag = flags[at : at + 1, :]
                news = []
                turned_over = jnp.zeros((rd, cd), F32)
                for g in range(groups):
                    k = block(g)
                    above, a, below = (rows[y + grow + i][k] for i in range(3))
                    if main:
                        ahead, behind = across(a, rims[0], y, g)
                    else:
                        ahead, behind = across(a, rims[1], at if y < 0 else at - rd, g)
                    falling = sink * a
                    rolled = pltpu.roll(falling, 1, 0)
                    arriving = jnp.where(first_sub, turned_over, rolled)
                    turned_over = rolled
                    new = (
                        (coef[0, at, k, :] * a + coef[1, at, k, :] * ahead)
                        + (coef[2, at, k, :] * behind + coef[3, at, k, :] * below)
                        + (coef[4, at, k, :] * above + flag * spread[b, k, :])
                        + (arriving - falling)
                    )
                    if not main:
                        new = new * keep[0 if y < 0 else 1]
                    if last:
                        flat_out[pl.ds(b * (nz * rd) + g * (rd * rd) + y, rd, stride=rd), :] = new
                    else:
                        dst[b, at, k, :] = new
                    news.append(new)
                if main:
                    fallen = falling[rd - 1 :, :]
                    here_row = (b, slice(y, y + 1), slice(None))
                    deposit[here_row] = fallen if stage == 0 else deposit[here_row] + fallen
                    fresh.append((y, news))
                elif -grow < y < rd + grow - 1:
                    outer.append((at if y < 0 else at - rd, news))
            if not last:
                col_out[2 * stage + 2, b] = pack(fresh)
                send_cols(2 * stage + 2, b)
            if outer:
                col_out[2 * stage + 3, b] = pack(outer)
                send_cols(2 * stage + 3, b)
            return 0

        lax.fori_loop(0, bins, one_bin, 0)

    for d in range(1, n_rows):
        band_copy(r, lax.rem(r + d, n_rows), d).wait_send()
    each(range(4), lambda side: wind_copy(side).wait_send())
    for i in range(4):

        @pl.when(has_corner[i])
        def _():
            diag_copy(i).wait_send()

    each((UP, DOWN), lambda side: flag_copy(side).wait_send())

    def drain(b, _):
        each((UP, DOWN), lambda side: row_copy(side, b).wait_send())
        for kind in range(2 * STEPS - 1):
            each((LEFT, RIGHT), lambda side: col_copy(kind, side, b).wait_send())
        return 0

    lax.fori_loop(0, bins, drain, 0)


def per_device(conc, nwp, lev_lo, frac, pick, corner_slot, corner_wt, settle, source_mask, profile):
    n_rows, n_cols = lax.axis_size("rows"), lax.axis_size("cols")
    bins, nz, rd, cd = conc.shape
    cap = pick.shape[3]
    slots = n_rows * cap
    columns = nwp.shape[2]
    tall = rd + 2 * (STEPS - 1)
    vmem = pl.BlockSpec(memory_space=pltpu.VMEM)
    smem = pl.BlockSpec(memory_space=pltpu.SMEM)
    return pl.pallas_call(
        functools.partial(kernel, n_rows, n_cols),
        out_shape=(
            jax.ShapeDtypeStruct(conc.shape, F32),
            jax.ShapeDtypeStruct((bins, rd, cd), F32),
        ),
        in_specs=[vmem] * 7 + [smem, vmem, vmem],
        out_specs=(vmem, vmem),
        scratch_shapes=[
            pltpu.VMEM((2 * nz, columns), BF16),
            pltpu.VMEM((columns, 4 * cap), BF16),
            pltpu.VMEM((slots, 128), BF16),
            pltpu.VMEM((slots, 128), BF16),
            pltpu.VMEM((128, slots), BF16),
            pltpu.VMEM(corner_wt.shape, F32),
            pltpu.VMEM((rd // 2, slots, 2 * cd), BF16),
            pltpu.VMEM((rd // 2, slots, 2 * cd), BF16),
            pltpu.VMEM((rd, 2 * nz, cd), F32),
            pltpu.VMEM((2, (2 * STEPS - 1) * nz, cd), BF16),
            pltpu.VMEM((2, (2 * STEPS - 1) * nz, cd), BF16),
            pltpu.VMEM((rd, cd), F32),
            pltpu.VMEM((2, rd, cd), F32),
            pltpu.VMEM((4, rd, cd), F32),
            pltpu.VMEM((2 * rd, cd), BF16),
            pltpu.VMEM((2, 2 * rd, cd), BF16),
            pltpu.VMEM((2, bins, STEPS * nz, cd), BF16),
            pltpu.VMEM((2, bins, STEPS * nz, cd), BF16),
            pltpu.VMEM((2 * STEPS - 1, bins, rd, cd), F32),
            pltpu.VMEM((2, 2 * STEPS - 1, bins, rd, cd), F32),
            pltpu.VMEM((5, tall, nz, cd), F32),
            pltpu.VMEM((bins, tall, nz, cd), F32),
            pltpu.VMEM((bins, tall, nz, cd), F32),
            pltpu.VMEM((bins, nz, cd), F32),
            pltpu.VMEM((2 * rd, cd), F32),
            pltpu.SemaphoreType.DMA((n_rows,)),
            pltpu.SemaphoreType.DMA((n_rows,)),
            pltpu.SemaphoreType.DMA((4,)),
            pltpu.SemaphoreType.DMA((4,)),
            pltpu.SemaphoreType.DMA((4,)),
            pltpu.SemaphoreType.DMA((4,)),
            pltpu.SemaphoreType.DMA((2,)),
            pltpu.SemaphoreType.DMA((2,)),
            pltpu.SemaphoreType.DMA((2, bins)),
            pltpu.SemaphoreType.DMA((2, bins)),
            pltpu.SemaphoreType.DMA((2 * STEPS - 1, 2, bins)),
            pltpu.SemaphoreType.DMA((2 * STEPS - 1, 2, bins)),
        ],
        compiler_params=pltpu.CompilerParams(
            collective_id=0, has_side_effects=True, vmem_limit_bytes=48 * 1024 * 1024
        ),
        cost_estimate=pl.CostEstimate(
            flops=10**9, bytes_accessed=6 * 10**6, transcendentals=0
        ),
        name="ash",
    )(
        conc,
        nwp,
        lev_lo.reshape(1, -1),
        frac.reshape(1, -1),
        pick,
        corner_slot,
        corner_wt,
        settle,
        source_mask,
        profile,
    )


def solution(mesh):
    placed = (
        P(None, None, "rows", "cols"),
        P(None, None, "rows"),
        P(),
        P(),
        P("rows", "cols", None, None),
        P(None, "rows", "cols"),
        P(None, "rows", "cols"),
        P(),
        P("rows", "cols"),
        P(),
    )
    return jax.shard_map(
        per_device,
        mesh=mesh,
        in_specs=placed,
        out_specs=(P(None, None, "rows", "cols"), P(None, "rows", "cols")),
        check_vma=False,
    )
```

time: 33.2 us -> 41.7 us (1.26)
  the two profiles are of different devices: /device:TPU:0 before, /device:TPU:1 now
where the time goes in v3:
time: 41.7 us; the launch traced here: 41.6 us
  Pallas kernels  37.2 us (89%)
  local copies, waits for them, and re-layouts  3.58 us (9%)
  between operations  0.79 us (2%)
    pallas_call x1, Pallas kernels, per_device(): pl.pallas_call(functools.partial(kernel, n_rows, n_cols), out_shape=(jax....  37.2 us
    unnamed x21, local copies, waits for them, and re-layouts  3.58 us

profile of v3, /device:TPU:1, one launch (start us, length us, event | category | flops | bytes accessed | tf_op | source)
XLA Modules:
  0.0 41.6 jit_solution(4191445377824762073)
XLA Ops:
  0.6 0.0 copy-start.5
  0.6 0.0 copy-start.4
  0.7 0.0 copy-start.8
  0.7 0.0 copy-start.2
  0.7 0.0 copy-start.1
  0.7 0.0 copy-start.3
  0.7 0.0 copy-start.7
  0.7 0.0 copy-start.6
  0.7 0.0 copy-start
  0.7 1.8 %copy.12.nwp = bf16[2,137,2048]{2,1,0:T(8,128)(2,1)S(1)} copy(bf16[2,137,2048]{2,0,1:T(2,128)(2,1)} %param.11) | data formatting | bytes 2244608 | tf_op args[1]
  2.5 0.0 copy-done.5
  2.5 0.0 copy-done.4
  2.5 0.0 copy-done.8
  2.5 0.0 copy-done.2
  2.5 0.0 copy-done.1
  2.6 0.0 copy-done.3
  2.6 0.0 copy-done.7
  2.6 0.0 copy-done.6
  2.6 0.0 copy-done
  2.6 37.2 %ash.1 = (f32[8,48,8,128]{3,2,1,0:T(8,128)S(1)}, f32[8,8,128]{2,1,0:T(8,128)S(1)}) custom-call(f32[8,48,8,128]{3,2,1,0:T(8,128)S(1)} %copy-done, bf16[2,137,2048]{2,1,0:T(8,128)(2,1)S(1)} %copy.12.nwp, s32[1,48]{1,0:T(1,128)S(1)} %bitcast.2, f32[1,48]{1,0:T(1,128)S(1)} %bitcast.3, s32[1,1,8,64]{3,2,1,0:T(8,128)S(1)} %copy-done.3, ...), custom_call_target="tpu_custom_call" | custom-call | flops 1000000000 | bytes 6000000 | tf_op jit(solution)/shard_map/ash/pallas_call | solution.py:555
  39.8 1.1 %copy.15 = f32[8,48,8,128]{3,2,1,0:T(8,128)} copy(f32[8,48,8,128]{3,2,1,0:T(8,128)S(1)} %get-tuple-element.4) | data formatting | bytes 3145728
  40.9 0.6 %copy.16 = f32[8,8,128]{2,1,0:T(8,128)} copy(f32[8,8,128]{2,1,0:T(8,128)S(1)} %get-tuple-element.5) | data formatting | bytes 65536
Async XLA Ops:
  0.6 1.9 %copy-start.5 = (f32[8,48]{1,0:T(8,128)S(1)}, f32[8,48]{1,0:T(8,128)}, u32[]{:S(2)}) copy-start(f32[8,48]{1,0:T(8,128)} %profile.1) | copy-start | bytes 4612
  0.6 1.9 %copy-start.4 = (s32[8,128]{1,0:T(8,128)S(1)}, s32[8,128]{1,0:T(8,128)}, u32[]{:S(2)}) copy-start(s32[8,128]{1,0:T(8,128)} %source_mask.1) | copy-start | bytes 12292
  0.7 1.9 %copy-start.8 = (f32[8]{0:T(128)S(1)}, f32[8]{0:T(128)}, u32[]{:S(2)}) copy-start(f32[8]{0:T(128)} %settle.1) | copy-start | bytes 100
  0.7 1.9 %copy-start.2 = (f32[4,8,128]{2,1,0:T(8,128)S(1)}, f32[4,8,128]{2,1,0:T(8,128)}, u32[]{:S(2)}) copy-start(f32[4,8,128]{2,1,0:T(8,128)} %corner_wt.1) | copy-start | bytes 49156
  0.7 1.9 %copy-start.1 = (s32[4,8,128]{2,1,0:T(8,128)S(1)}, s32[4,8,128]{2,1,0:T(8,128)}, u32[]{:S(2)}) copy-start(s32[4,8,128]{2,1,0:T(8,128)} %corner_slot.1) | copy-start | bytes 49156
  0.7 1.9 %copy-start.3 = (s32[1,1,8,64]{3,2,1,0:T(8,128)S(1)}, s32[1,1,8,64]{3,2,1,0:T(8,128)}, u32[]{:S(2)}) copy-start(s32[1,1,8,64]{3,2,1,0:T(8,128)} %pick.1) | copy-start | bytes 6148
  0.7 1.9 %copy-start.7 = (f32[48]{0:T(128)S(1)}, f32[48]{0:T(128)}, u32[]{:S(2)}) copy-start(f32[48]{0:T(128)} %param.13) | copy-start | bytes 580
  0.7 1.9 %copy-start.6 = (s32[48]{0:T(128)S(1)}, s32[48]{0:T(128)}, u32[]{:S(2)}) copy-start(s32[48]{0:T(128)} %param.12) | copy-start | bytes 580
  0.7 1.9 %copy-start = (f32[8,48,8,128]{3,2,1,0:T(8,128)S(1)}, f32[8,48,8,128]{3,2,1,0:T(8,128)}, u32[]{:S(2)}) copy-start(f32[8,48,8,128]{3,2,1,0:T(8,128)} %conc.1) | copy-start | bytes 4718596

commit v4 on v2

--- a/solution.py
+++ b/solution.py
@@ -198,6 +198,16 @@
 
     lax.fori_loop(0, bins, first_pack, 0)
 
+    pl.semaphore_wait(
+        barrier, n_rows - 1 + has[LEFT].astype(jnp.int32) + has[RIGHT].astype(jnp.int32)
+    )
+
+    def first_send(b, _):
+        send_halo(0, b)
+        return 0
+
+    lax.fori_loop(0, bins, first_send, 0)
+
     diag = lax.broadcasted_iota(jnp.int32, (nz, nz), 0) == lax.broadcasted_iota(
         jnp.int32, (nz, nz), 1
     )
@@ -211,14 +221,10 @@
     )
     interp_hi = interp.astype(BF16)
     rest = interp - interp_hi.astype(F32)
-    interp_mid = rest.astype(BF16)
-    interp_lo = (rest - interp_mid.astype(F32)).astype(BF16)
-    parts = jnp.concatenate([interp_hi, interp_mid, interp_lo], axis=0)
+    parts = jnp.concatenate([interp_hi, rest.astype(BF16)], axis=0)
     for f in range(2):
         mixed = jnp.dot(parts, nwp[f], preferred_element_type=F32)
-        levels[f * nz : (f + 1) * nz, :] = (
-            mixed[:nz] + mixed[nz : 2 * nz] + mixed[2 * nz :]
-        ).astype(BF16)
+        levels[f * nz : (f + 1) * nz, :] = (mixed[:nz] + mixed[nz:]).astype(BF16)
 
     def band_copy(source, dest, d):
         return pltpu.make_async_remote_copy(
@@ -249,17 +255,8 @@
         return 0
 
     lax.fori_loop(0, n_rows // per, choose, 0)
-    pl.semaphore_wait(
-        barrier, n_rows - 1 + has[LEFT].astype(jnp.int32) + has[RIGHT].astype(jnp.int32)
-    )
     for d in range(1, n_rows):
         band_copy(r, lax.rem(r + d, n_rows), d).start()
-
-    def first_send(b, _):
-        send_halo(0, b)
-        return 0
-
-    lax.fori_loop(0, bins, first_send, 0)
 
     weights = corner_wt[...]
     norm_wt[...] = weights / (weights[0] + weights[1] + weights[2] + weights[3])
@@ -283,6 +280,14 @@
 
     lax.fori_loop(0, (rd // 2) * (slots // chunk), fill_table, 0)
 
+    diag = lax.broadcasted_iota(jnp.int32, (nz, nz), 0) == lax.broadcasted_iota(
+        jnp.int32, (nz, nz), 1
+    )
+    for b in range(bins):
+        column = jnp.sum(jnp.where(diag, profile[b : b + 1, :], 0.0), axis=1, keepdims=True)
+        spread[b] = jnp.broadcast_to(column, (nz, cd))
+    flags[...] = source_mask[...].astype(F32)
+
     own = pl.ds(pl.multiple_of(r * cap, cap), cap)
     got[own, :] = sent[own, :]
     for d in range(1, n_rows):
@@ -307,11 +312,12 @@
         def _():
             wind_copy(side).start()
 
-    for side in range(4):
-
-        @pl.when(has[side])
-        def _():
-            wind_arrival(side).wait_recv()
+    def wind_wait(sides):
+        for side in sides:
+
+            @pl.when(has[side])
+            def _():
+                wind_arrival(side).wait_recv()
 
     def across(plane, rim, y, g):
         rim = pltpu.roll(rim, cd - 2 * (y * groups + g) - 1, 1)
@@ -319,18 +325,23 @@
         behind = jnp.where(first_lane, rim, pltpu.roll(plane, 1, 1))
         return ahead, behind
 
+    wind_wait((LEFT, RIGHT))
     wind_rim = unpack(wind_col_in[0], wind_col_in[1])
-    wind_rows = (
-        [wind_row_in[UP].astype(F32)]
-        + [winds[y, nz:, :] for y in range(rd)]
-        + [wind_row_in[DOWN].astype(F32)]
-    )
-    for y in range(rd):
+
+    def north_row(y):
+        if y < 0:
+            return wind_row_in[UP].astype(F32)
+        return winds[y, nz:, :] if y < rd else wind_row_in[DOWN].astype(F32)
+
+    for y in [*range(1, rd - 1), 0, rd - 1]:
+        if y == 0:
+            wind_wait((UP, DOWN))
+        near = [north_row(y + i) for i in (-1, 0, 1)]
         for g in range(groups):
             k = block(g)
             u = winds[y, k, :]
             u_ahead, u_behind = across(u, wind_rim, y, g)
-            v_above, v, v_below = (wind_rows[y + i][k] for i in range(3))
+            v_above, v, v_below = (row[k] for row in near)
             right, left = 0.5 * (u + u_ahead), 0.5 * (u + u_behind)
             down, up = 0.5 * (v + v_below), 0.5 * (v + v_above)
             coef[0, y, k, :] = (
@@ -345,13 +356,6 @@
             coef[3, y, k, :] = KAPPA - jnp.minimum(down, 0.0)
             coef[4, y, k, :] = KAPPA + jnp.maximum(up, 0.0)
 
-    diag = lax.broadcasted_iota(jnp.int32, (nz, nz), 0) == lax.broadcasted_iota(
-        jnp.int32, (nz, nz), 1
-    )
-    for b in range(bins):
-        column = jnp.sum(jnp.where(diag, profile[b : b + 1, :], 0.0), axis=1, keepdims=True)
-        spread[b] = jnp.broadcast_to(column, (nz, cd))
-    flags[...] = source_mask[...].astype(F32)
     flat_out = out.reshape(bins * nz * rd, cd)
     for stage in range(STEPS):
         src = (state_a, state_b)[stage % 2]

time: 33.2 us -> 34.1 us (1.027)
  Pallas kernels: 28.7 us -> 29.6 us
    pallas_call x1, Pallas kernels: 28.7 us -> 29.6 us  [per_device(): pl.pallas_call(functools.partial(kernel, n_rows, n_cols), out_shape=(jax....]
where the time goes in v4:
time: 34.1 us; the launch traced here: 34 us
  Pallas kernels  29.6 us (87%)
  local copies, waits for them, and re-layouts  3.58 us (10%)
  between operations  0.79 us (2%)
    pallas_call x1, Pallas kernels, per_device(): pl.pallas_call(functools.partial(kernel, n_rows, n_cols), out_shape=(jax....  29.6 us
    unnamed x21, local copies, waits for them, and re-layouts  3.58 us

profile of v4, /device:TPU:0, one launch (start us, length us, event | category | flops | bytes accessed | tf_op | source)
XLA Modules:
  0.0 34.0 jit_solution(12856196892730828386)
XLA Ops:
  0.6 0.0 copy-start.5
  0.6 0.0 copy-start.4
  0.7 0.0 copy-start.8
  0.7 0.0 copy-start.2
  0.7 0.0 copy-start.1
  0.7 0.0 copy-start.3
  0.7 0.0 copy-start.7
  0.7 0.0 copy-start.6
  0.7 0.0 copy-start
  0.7 1.8 %copy.12.nwp = bf16[2,137,2048]{2,1,0:T(8,128)(2,1)S(1)} copy(bf16[2,137,2048]{2,0,1:T(2,128)(2,1)} %param.11) | data formatting | bytes 2244608 | tf_op args[1]
  2.5 0.0 copy-done.5
  2.5 0.0 copy-done.4
  2.5 0.0 copy-done.8
  2.5 0.0 copy-done.2
  2.5 0.0 copy-done.1
  2.6 0.0 copy-done.3
  2.6 0.0 copy-done.7
  2.6 0.0 copy-done.6
  2.6 0.0 copy-done
  2.6 29.6 %ash.1 = (f32[8,48,8,128]{3,2,1,0:T(8,128)S(1)}, f32[8,8,128]{2,1,0:T(8,128)S(1)}) custom-call(f32[8,48,8,128]{3,2,1,0:T(8,128)S(1)} %copy-done, bf16[2,137,2048]{2,1,0:T(8,128)(2,1)S(1)} %copy.12.nwp, s32[1,48]{1,0:T(1,128)S(1)} %bitcast.2, f32[1,48]{1,0:T(1,128)S(1)} %bitcast.3, s32[1,1,8,64]{3,2,1,0:T(8,128)S(1)} %copy-done.3, ...), custom_call_target="tpu_custom_call" | custom-call | flops 1000000000 | bytes 6000000 | tf_op jit(solution)/shard_map/ash/pallas_call | solution.py:441
  32.2 1.1 %copy.15 = f32[8,48,8,128]{3,2,1,0:T(8,128)} copy(f32[8,48,8,128]{3,2,1,0:T(8,128)S(1)} %get-tuple-element.4) | data formatting | bytes 3145728
  33.3 0.6 %copy.16 = f32[8,8,128]{2,1,0:T(8,128)} copy(f32[8,8,128]{2,1,0:T(8,128)S(1)} %get-tuple-element.5) | data formatting | bytes 65536
Async XLA Ops:
  0.6 1.9 %copy-start.5 = (f32[8,48]{1,0:T(8,128)S(1)}, f32[8,48]{1,0:T(8,128)}, u32[]{:S(2)}) copy-start(f32[8,48]{1,0:T(8,128)} %profile.1) | copy-start | bytes 4612
  0.6 1.9 %copy-start.4 = (s32[8,128]{1,0:T(8,128)S(1)}, s32[8,128]{1,0:T(8,128)}, u32[]{:S(2)}) copy-start(s32[8,128]{1,0:T(8,128)} %source_mask.1) | copy-start | bytes 12292
  0.7 1.9 %copy-start.8 = (f32[8]{0:T(128)S(1)}, f32[8]{0:T(128)}, u32[]{:S(2)}) copy-start(f32[8]{0:T(128)} %settle.1) | copy-start | bytes 100
  0.7 1.9 %copy-start.2 = (f32[4,8,128]{2,1,0:T(8,128)S(1)}, f32[4,8,128]{2,1,0:T(8,128)}, u32[]{:S(2)}) copy-start(f32[4,8,128]{2,1,0:T(8,128)} %corner_wt.1) | copy-start | bytes 49156
  0.7 1.9 %copy-start.1 = (s32[4,8,128]{2,1,0:T(8,128)S(1)}, s32[4,8,128]{2,1,0:T(8,128)}, u32[]{:S(2)}) copy-start(s32[4,8,128]{2,1,0:T(8,128)} %corner_slot.1) | copy-start | bytes 49156
  0.7 1.9 %copy-start.3 = (s32[1,1,8,64]{3,2,1,0:T(8,128)S(1)}, s32[1,1,8,64]{3,2,1,0:T(8,128)}, u32[]{:S(2)}) copy-start(s32[1,1,8,64]{3,2,1,0:T(8,128)} %pick.1) | copy-start | bytes 6148
  0.7 1.9 %copy-start.7 = (f32[48]{0:T(128)S(1)}, f32[48]{0:T(128)}, u32[]{:S(2)}) copy-start(f32[48]{0:T(128)} %param.13) | copy-start | bytes 580
  0.7 1.9 %copy-start.6 = (s32[48]{0:T(128)S(1)}, s32[48]{0:T(128)}, u32[]{:S(2)}) copy-start(s32[48]{0:T(128)} %param.12) | copy-start | bytes 580
  0.7 1.9 %copy-start = (f32[8,48,8,128]{3,2,1,0:T(8,128)S(1)}, f32[8,48,8,128]{3,2,1,0:T(8,128)}, u32[]{:S(2)}) copy-start(f32[8,48,8,128]{3,2,1,0:T(8,128)} %conc.1) | copy-start | bytes 4718596

commit v5 on v4

--- a/solution.py
+++ b/solution.py
@@ -9,6 +9,7 @@
 
 STEPS = 3
 KAPPA = 0.05
+SPAN = 4
 MESH = pl.DeviceIdType.MESH
 UP, DOWN, LEFT, RIGHT = range(4)
 BF16 = jnp.bfloat16
@@ -116,12 +117,13 @@
     def unpack(left, right):
         return jnp.where(odd, pltpu.roll(left, 1, 1), pltpu.roll(right, cd - 1, 1))
 
-    def halo_copy(stage, side, b):
+    def halo_copy(stage, side, b, size):
         other = side ^ 1
+        some = pl.ds(b, size)
         if side < 2:
-            src, dst = row_out.at[stage, side, b], row_in.at[stage, other, b]
+            src, dst = row_out.at[stage, side, some], row_in.at[stage, other, some]
         else:
-            src, dst = col_out.at[stage, b], col_in.at[stage, other - 2, b]
+            src, dst = col_out.at[stage, some], col_in.at[stage, other - 2, some]
         return pltpu.make_async_remote_copy(
             src_ref=src,
             dst_ref=dst,
@@ -131,11 +133,12 @@
             device_id_type=MESH,
         )
 
-    def halo_arrival(stage, side, b):
+    def halo_arrival(stage, side, b, size):
+        some = pl.ds(b, size)
         if side < 2:
-            src, dst = row_out.at[stage, side, b], row_in.at[stage, side, b]
+            src, dst = row_out.at[stage, side, some], row_in.at[stage, side, some]
         else:
-            src, dst = col_out.at[stage, b], col_in.at[stage, side - 2, b]
+            src, dst = col_out.at[stage, some], col_in.at[stage, side - 2, some]
         return pltpu.make_async_remote_copy(
             src_ref=src,
             dst_ref=dst,
@@ -174,12 +177,12 @@
             device_id_type=MESH,
         )
 
-    def send_halo(stage, b):
+    def send_halo(stage, b, size):
         for side in range(4):
 
             @pl.when(has[side])
             def _():
-                halo_copy(stage, side, b).start()
+                halo_copy(stage, side, b, size).start()
 
     flat_conc = conc.reshape(bins * nz * rd, cd)
 
@@ -198,16 +201,6 @@
 
     lax.fori_loop(0, bins, first_pack, 0)
 
-    pl.semaphore_wait(
-        barrier, n_rows - 1 + has[LEFT].astype(jnp.int32) + has[RIGHT].astype(jnp.int32)
-    )
-
-    def first_send(b, _):
-        send_halo(0, b)
-        return 0
-
-    lax.fori_loop(0, bins, first_send, 0)
-
     diag = lax.broadcasted_iota(jnp.int32, (nz, nz), 0) == lax.broadcasted_iota(
         jnp.int32, (nz, nz), 1
     )
@@ -255,8 +248,13 @@
         return 0
 
     lax.fori_loop(0, n_rows // per, choose, 0)
+
+    pl.semaphore_wait(
+        barrier, n_rows - 1 + has[LEFT].astype(jnp.int32) + has[RIGHT].astype(jnp.int32)
+    )
     for d in range(1, n_rows):
         band_copy(r, lax.rem(r + d, n_rows), d).start()
+    send_halo(0, 0, bins)
 
     weights = corner_wt[...]
     norm_wt[...] = weights / (weights[0] + weights[1] + weights[2] + weights[3])
@@ -363,12 +361,6 @@
         last = stage == STEPS - 1
 
         def one_bin(b, _):
-            for side in range(4):
-
-                @pl.when(has[side])
-                def _():
-                    halo_arrival(stage, side, b).wait_recv()
-
             rim = unpack(col_in[stage, 0, b], col_in[stage, 1, b])
             sink = settle[b]
             rows = (
@@ -409,10 +401,27 @@
             if not last:
                 row_out[stage + 1, DOWN, b] = jnp.concatenate(fresh[-1], axis=0).astype(BF16)
                 col_out[stage + 1, b] = pack(fresh)
-                send_halo(stage + 1, b)
             return 0
 
-        lax.fori_loop(0, bins, one_bin, 0)
+        size = bins if stage == 0 else SPAN
+
+        def one_span(i, _):
+            for side in range(4):
+
+                @pl.when(has[side])
+                def _():
+                    halo_arrival(stage, side, i * size, size).wait_recv()
+
+            def one_part(j, _):
+                first = i * size + j * SPAN
+                lax.fori_loop(first, first + SPAN, one_bin, 0)
+                if not last:
+                    send_halo(stage + 1, first, SPAN)
+                return 0
+
+            return lax.fori_loop(0, size // SPAN, one_part, 0)
+
+        lax.fori_loop(0, bins // size, one_span, 0)
 
     for d in range(1, n_rows):
         band_copy(r, lax.rem(r + d, n_rows), d).wait_send()
@@ -422,12 +431,10 @@
         def _():
             wind_copy(side).wait_send()
 
-            def drain(b, _):
-                for stage in range(STEPS):
-                    halo_copy(stage, side, b).wait_send()
-                return 0
-
-            lax.fori_loop(0, bins, drain, 0)
+            halo_copy(0, side, 0, bins).wait_send()
+            for stage in range(1, STEPS):
+                for b in range(0, bins, SPAN):
+                    halo_copy(stage, side, b, SPAN).wait_send()
 
 
 def per_device(conc, nwp, lev_lo, frac, pick, corner_slot, corner_wt, settle, source_mask, profile):

time: 34.1 us -> 36.2 us (1.062)
  Pallas kernels: 29.6 us -> 31.4 us
    pallas_call x1, Pallas kernels: 29.6 us -> 31.4 us  [per_device(): pl.pallas_call(functools.partial(kernel, n_rows, n_cols), out_shape=(jax....]
where the time goes in v5:
time: 36.2 us; the launch traced here: 35.8 us
  Pallas kernels  31.4 us (87%)
  local copies, waits for them, and re-layouts  3.58 us (10%)
  between operations  0.79 us (2%)
    pallas_call x1, Pallas kernels, per_device(): pl.pallas_call(functools.partial(kernel, n_rows, n_cols), out_shape=(jax....  31.4 us
    unnamed x21, local copies, waits for them, and re-layouts  3.58 us

profile of v5, /device:TPU:0, one launch (start us, length us, event | category | flops | bytes accessed | tf_op | source)
XLA Modules:
  0.0 35.8 jit_solution(4769935015721042575)
XLA Ops:
  0.6 0.0 copy-start.5
  0.6 0.0 copy-start.4
  0.7 0.0 copy-start.8
  0.7 0.0 copy-start.2
  0.7 0.0 copy-start.1
  0.7 0.0 copy-start.3
  0.7 0.0 copy-start.7
  0.7 0.0 copy-start.6
  0.7 0.0 copy-start
  0.7 1.8 %copy.12.nwp = bf16[2,137,2048]{2,1,0:T(8,128)(2,1)S(1)} copy(bf16[2,137,2048]{2,0,1:T(2,128)(2,1)} %param.11) | data formatting | bytes 2244608 | tf_op args[1]
  2.5 0.0 copy-done.5
  2.5 0.0 copy-done.4
  2.5 0.0 copy-done.8
  2.5 0.0 copy-done.2
  2.5 0.0 copy-done.1
  2.6 0.0 copy-done.3
  2.6 0.0 copy-done.7
  2.6 0.0 copy-done.6
  2.6 0.0 copy-done
  2.6 31.4 %ash.1 = (f32[8,48,8,128]{3,2,1,0:T(8,128)S(1)}, f32[8,8,128]{2,1,0:T(8,128)S(1)}) custom-call(f32[8,48,8,128]{3,2,1,0:T(8,128)S(1)} %copy-done, bf16[2,137,2048]{2,1,0:T(8,128)(2,1)S(1)} %copy.12.nwp, s32[1,48]{1,0:T(1,128)S(1)} %bitcast.2, f32[1,48]{1,0:T(1,128)S(1)} %bitcast.3, s32[1,1,8,64]{3,2,1,0:T(8,128)S(1)} %copy-done.3, ...), custom_call_target="tpu_custom_call" | custom-call | flops 1000000000 | bytes 6000000 | tf_op jit(solution)/shard_map/ash/pallas_call | solution.py:448
  34.0 1.1 %copy.15 = f32[8,48,8,128]{3,2,1,0:T(8,128)} copy(f32[8,48,8,128]{3,2,1,0:T(8,128)S(1)} %get-tuple-element.4) | data formatting | bytes 3145728
  35.2 0.6 %copy.16 = f32[8,8,128]{2,1,0:T(8,128)} copy(f32[8,8,128]{2,1,0:T(8,128)S(1)} %get-tuple-element.5) | data formatting | bytes 65536
Async XLA Ops:
  0.6 1.9 %copy-start.5 = (f32[8,48]{1,0:T(8,128)S(1)}, f32[8,48]{1,0:T(8,128)}, u32[]{:S(2)}) copy-start(f32[8,48]{1,0:T(8,128)} %profile.1) | copy-start | bytes 4612
  0.6 1.9 %copy-start.4 = (s32[8,128]{1,0:T(8,128)S(1)}, s32[8,128]{1,0:T(8,128)}, u32[]{:S(2)}) copy-start(s32[8,128]{1,0:T(8,128)} %source_mask.1) | copy-start | bytes 12292
  0.7 1.9 %copy-start.8 = (f32[8]{0:T(128)S(1)}, f32[8]{0:T(128)}, u32[]{:S(2)}) copy-start(f32[8]{0:T(128)} %settle.1) | copy-start | bytes 100
  0.7 1.9 %copy-start.2 = (f32[4,8,128]{2,1,0:T(8,128)S(1)}, f32[4,8,128]{2,1,0:T(8,128)}, u32[]{:S(2)}) copy-start(f32[4,8,128]{2,1,0:T(8,128)} %corner_wt.1) | copy-start | bytes 49156
  0.7 1.9 %copy-start.1 = (s32[4,8,128]{2,1,0:T(8,128)S(1)}, s32[4,8,128]{2,1,0:T(8,128)}, u32[]{:S(2)}) copy-start(s32[4,8,128]{2,1,0:T(8,128)} %corner_slot.1) | copy-start | bytes 49156
  0.7 1.9 %copy-start.3 = (s32[1,1,8,64]{3,2,1,0:T(8,128)S(1)}, s32[1,1,8,64]{3,2,1,0:T(8,128)}, u32[]{:S(2)}) copy-start(s32[1,1,8,64]{3,2,1,0:T(8,128)} %pick.1) | copy-start | bytes 6148
  0.7 1.9 %copy-start.7 = (f32[48]{0:T(128)S(1)}, f32[48]{0:T(128)}, u32[]{:S(2)}) copy-start(f32[48]{0:T(128)} %param.13) | copy-start | bytes 580
  0.7 1.9 %copy-start.6 = (s32[48]{0:T(128)S(1)}, s32[48]{0:T(128)}, u32[]{:S(2)}) copy-start(s32[48]{0:T(128)} %param.12) | copy-start | bytes 580
  0.7 1.9 %copy-start = (f32[8,48,8,128]{3,2,1,0:T(8,128)S(1)}, f32[8,48,8,128]{3,2,1,0:T(8,128)}, u32[]{:S(2)}) copy-start(f32[8,48,8,128]{3,2,1,0:T(8,128)} %conc.1) | copy-start | bytes 4718596

commit v6 on v4

--- a/solution.py
+++ b/solution.py
@@ -198,16 +198,6 @@
 
     lax.fori_loop(0, bins, first_pack, 0)
 
-    pl.semaphore_wait(
-        barrier, n_rows - 1 + has[LEFT].astype(jnp.int32) + has[RIGHT].astype(jnp.int32)
-    )
-
-    def first_send(b, _):
-        send_halo(0, b)
-        return 0
-
-    lax.fori_loop(0, bins, first_send, 0)
-
     diag = lax.broadcasted_iota(jnp.int32, (nz, nz), 0) == lax.broadcasted_iota(
         jnp.int32, (nz, nz), 1
     )
@@ -255,8 +245,18 @@
         return 0
 
     lax.fori_loop(0, n_rows // per, choose, 0)
+    pl.semaphore_wait(
+        barrier, n_rows - 1 + has[LEFT].astype(jnp.int32) + has[RIGHT].astype(jnp.int32)
+    )
     for d in range(1, n_rows):
         band_copy(r, lax.rem(r + d, n_rows), d).start()
+
+    def first_send(b, _):
+        send_halo(0, b)
+        return 0
+
+    lax.fori_loop(0, bins, first_send, 0)
+
 
     weights = corner_wt[...]
     norm_wt[...] = weights / (weights[0] + weights[1] + weights[2] + weights[3])
@@ -368,6 +368,7 @@
                 @pl.when(has[side])
                 def _():
                     halo_arrival(stage, side, b).wait_recv()
+                    halo_copy(stage, side, b).wait_send()
 
             rim = unpack(col_in[stage, 0, b], col_in[stage, 1, b])
             sink = settle[b]
@@ -421,13 +422,6 @@
         @pl.when(has[side])
         def _():
             wind_copy(side).wait_send()
-
-            def drain(b, _):
-                for stage in range(STEPS):
-                    halo_copy(stage, side, b).wait_send()
-                return 0
-
-            lax.fori_loop(0, bins, drain, 0)
 
 
 def per_device(conc, nwp, lev_lo, frac, pick, corner_slot, corner_wt, settle, source_mask, profile):

time: 34.1 us -> 32.6 us (0.956)
  Pallas kernels: 29.6 us -> 28.1 us
    pallas_call x1, Pallas kernels: 29.6 us -> 28.1 us  [per_device(): pl.pallas_call(functools.partial(kernel, n_rows, n_cols), out_shape=(jax....]
where the time goes in v6:
time: 32.6 us; the launch traced here: 32.5 us
  Pallas kernels  28.1 us (86%)
  local copies, waits for them, and re-layouts  3.58 us (11%)
  between operations  0.79 us (2%)
    pallas_call x1, Pallas kernels, per_device(): pl.pallas_call(functools.partial(kernel, n_rows, n_cols), out_shape=(jax....  28.1 us
    unnamed x21, local copies, waits for them, and re-layouts  3.58 us

profile of v6, /device:TPU:0, one launch (start us, length us, event | category | flops | bytes accessed | tf_op | source)
XLA Modules:
  0.0 32.5 jit_solution(4055093142640348970)
XLA Ops:
  0.6 0.0 copy-start.5
  0.6 0.0 copy-start.4
  0.7 0.0 copy-start.8
  0.7 0.0 copy-start.2
  0.7 0.0 copy-start.1
  0.7 0.0 copy-start.3
  0.7 0.0 copy-start.7
  0.7 0.0 copy-start.6
  0.7 0.0 copy-start
  0.7 1.8 %copy.12.nwp = bf16[2,137,2048]{2,1,0:T(8,128)(2,1)S(1)} copy(bf16[2,137,2048]{2,0,1:T(2,128)(2,1)} %param.11) | data formatting | bytes 2244608 | tf_op args[1]
  2.5 0.0 copy-done.5
  2.5 0.0 copy-done.4
  2.5 0.0 copy-done.8
  2.5 0.0 copy-done.2
  2.5 0.0 copy-done.1
  2.6 0.0 copy-done.3
  2.6 0.0 copy-done.7
  2.6 0.0 copy-done.6
  2.6 0.0 copy-done
  2.6 28.1 %ash.1 = (f32[8,48,8,128]{3,2,1,0:T(8,128)S(1)}, f32[8,8,128]{2,1,0:T(8,128)S(1)}) custom-call(f32[8,48,8,128]{3,2,1,0:T(8,128)S(1)} %copy-done, bf16[2,137,2048]{2,1,0:T(8,128)(2,1)S(1)} %copy.12.nwp, s32[1,48]{1,0:T(1,128)S(1)} %bitcast.2, f32[1,48]{1,0:T(1,128)S(1)} %bitcast.3, s32[1,1,8,64]{3,2,1,0:T(8,128)S(1)} %copy-done.3, ...), custom_call_target="tpu_custom_call" | custom-call | flops 1000000000 | bytes 6000000 | tf_op jit(solution)/shard_map/ash/pallas_call | solution.py:435
  30.7 1.1 %copy.15 = f32[8,48,8,128]{3,2,1,0:T(8,128)} copy(f32[8,48,8,128]{3,2,1,0:T(8,128)S(1)} %get-tuple-element.4) | data formatting | bytes 3145728
  31.9 0.6 %copy.16 = f32[8,8,128]{2,1,0:T(8,128)} copy(f32[8,8,128]{2,1,0:T(8,128)S(1)} %get-tuple-element.5) | data formatting | bytes 65536
Async XLA Ops:
  0.6 1.9 %copy-start.5 = (f32[8,48]{1,0:T(8,128)S(1)}, f32[8,48]{1,0:T(8,128)}, u32[]{:S(2)}) copy-start(f32[8,48]{1,0:T(8,128)} %profile.1) | copy-start | bytes 4612
  0.6 1.9 %copy-start.4 = (s32[8,128]{1,0:T(8,128)S(1)}, s32[8,128]{1,0:T(8,128)}, u32[]{:S(2)}) copy-start(s32[8,128]{1,0:T(8,128)} %source_mask.1) | copy-start | bytes 12292
  0.7 1.9 %copy-start.8 = (f32[8]{0:T(128)S(1)}, f32[8]{0:T(128)}, u32[]{:S(2)}) copy-start(f32[8]{0:T(128)} %settle.1) | copy-start | bytes 100
  0.7 1.9 %copy-start.2 = (f32[4,8,128]{2,1,0:T(8,128)S(1)}, f32[4,8,128]{2,1,0:T(8,128)}, u32[]{:S(2)}) copy-start(f32[4,8,128]{2,1,0:T(8,128)} %corner_wt.1) | copy-start | bytes 49156
  0.7 1.9 %copy-start.1 = (s32[4,8,128]{2,1,0:T(8,128)S(1)}, s32[4,8,128]{2,1,0:T(8,128)}, u32[]{:S(2)}) copy-start(s32[4,8,128]{2,1,0:T(8,128)} %corner_slot.1) | copy-start | bytes 49156
  0.7 1.9 %copy-start.3 = (s32[1,1,8,64]{3,2,1,0:T(8,128)S(1)}, s32[1,1,8,64]{3,2,1,0:T(8,128)}, u32[]{:S(2)}) copy-start(s32[1,1,8,64]{3,2,1,0:T(8,128)} %pick.1) | copy-start | bytes 6148
  0.7 1.9 %copy-start.7 = (f32[48]{0:T(128)S(1)}, f32[48]{0:T(128)}, u32[]{:S(2)}) copy-start(f32[48]{0:T(128)} %param.13) | copy-start | bytes 580
  0.7 1.9 %copy-start.6 = (s32[48]{0:T(128)S(1)}, s32[48]{0:T(128)}, u32[]{:S(2)}) copy-start(s32[48]{0:T(128)} %param.12) | copy-start | bytes 580
  0.7 1.9 %copy-start = (f32[8,48,8,128]{3,2,1,0:T(8,128)S(1)}, f32[8,48,8,128]{3,2,1,0:T(8,128)}, u32[]{:S(2)}) copy-start(f32[8,48,8,128]{3,2,1,0:T(8,128)} %conc.1) | copy-start | bytes 4718596
